TPU v7x, 128 devices: a whole 4x4x4 slice. The times are simulated.
128 devices in a mesh: seq: 32 (over x, y, core), head: 4 (over z).
Axes of the slice: x: 4, y: 4, z: 4, core: 2. Of those that a mesh axis runs over, the one named last changes fastest.
Arguments:
- query: bfloat16 [32768, 256], P('seq', 'head'), may hold values from -6 to 6
- key_feat: bfloat16 [32768, 256], P('seq', 'head'), may hold values from -6 to 6
- values: bfloat16 [32768, 2048], P('seq', 'head'), may hold values from -6 to 6
- conv_w: float32 [3, 2048], P(None, 'head'), may hold values from -3 to 3
- gain: float32 [2048], P('head'), may hold values from 0.1 to 1.9
- w_out: bfloat16 [4096, 2048], P(None, 'head'), may hold values from -0.125 to 0.125
- cotangent: bfloat16 [32768, 4096], P('seq', 'head'), may hold values from -6 to 6
Outputs:
- mixed: bfloat16 [32768, 4096], P('seq', 'head')
- grad_query: bfloat16 [32768, 256], P('seq', 'head')
- grad_key: bfloat16 [32768, 256], P('seq', 'head')
- grad_values: bfloat16 [32768, 2048], P('seq', 'head')
- grad_w_out: bfloat16 [4096, 2048], P('seq', 'head')
All inputs are finite; a program needn't handle non-finite values.
Results may differ from a plain program's by a relative error of at most 0.024.
Values may be sent and summed in bfloat16 or wider, within the bound.
A program may use at most 192 MiB of HBM per device.

v0:
```python
import jax
import jax.numpy as jnp
from jax import lax
from jax.sharding import PartitionSpec as P

FD = 16
BLOCK = 256


EPSILON = 1e-05


def from_behind(block, axis, distance):
    devices = range(lax.axis_size(axis))
    route = [(i - distance, i) for i in devices if i - distance in devices]
    return lax.ppermute(block, axis, route)


def entering(part, axis, combine, identity):
    place = lax.axis_index(axis)
    gathered = lax.all_gather(part, axis)
    state = jnp.zeros_like(part) + jnp.asarray(identity, part.dtype)

    def entering_one(turn, state):
        return combine(state, lax.dynamic_index_in_dim(gathered, turn, 0, False))

    return lax.fori_loop(0, place, entering_one, state)


def carried_in(x, axis, join, neutral):
    count = lax.axis_size(axis)
    place = lax.axis_index(axis)
    ahead = count - 1 - place
    gathered = lax.all_gather(x.astype(jnp.bfloat16), axis)
    state = jnp.zeros_like(x) + jnp.asarray(neutral, x.dtype)

    def carried_one(turn, state):
        source = count - 1 - turn
        return join(state, lax.dynamic_index_in_dim(gathered, source, 0, False).astype(x.dtype))

    return lax.fori_loop(0, ahead, carried_one, state)


def features(inputs, width):
    first = width ** (-0.25)
    second = (2.0 * width) ** (-0.5)
    outer = (inputs[..., :, None] * inputs[..., None, :]).reshape(
        inputs.shape[:-1] + (width * width,)
    )
    ones = jnp.ones(inputs.shape[:-1] + (1,), inputs.dtype)
    return jnp.concatenate([ones, inputs * first, outer * second], axis=-1)


def feature_grad(upstream, inputs, width):
    first = width ** (-0.25)
    second = (2.0 * width) ** (-0.5)
    linear = upstream[..., 1 : 1 + width] * first
    square = upstream[..., 1 + width :].reshape(upstream.shape[:-1] + (width, width)) * second
    return (
        linear
        + jnp.einsum("...ij,...j->...i", square, inputs)
        + jnp.einsum("...ji,...j->...i", square, inputs)
    )


def to_blocks(array, block, heads):
    rows, cols = array.shape
    return array.reshape(rows // block, block, heads, cols // heads).transpose(0, 2, 1, 3)


def from_blocks(array):
    count, heads, block, cols = array.shape
    return array.transpose(0, 2, 1, 3).reshape(count * block, heads * cols)


def exclusive_forward(states):
    totals = jnp.cumsum(states, axis=0)
    return jnp.concatenate([jnp.zeros_like(states[:1]), totals[:-1]], axis=0)


def exclusive_backward(states):
    totals = jnp.cumsum(states[::-1], axis=0)[::-1]
    return jnp.concatenate([totals[1:], jnp.zeros_like(states[:1])], axis=0)


def add_states(earlier, later):
    return earlier + later


def on_device(query, key_feat, values, conv_w, gain, w_out, cotangent):
    f32 = jnp.float32
    bf16 = jnp.bfloat16
    heads = query.shape[1] // FD
    rows = values.shape[0]
    span = conv_w.shape[0] - 1
    mask = jnp.tril(jnp.ones((BLOCK, BLOCK), f32))
    tail = values[rows - span :]
    rim = from_behind(tail, "seq", 1)
    extended = jnp.concatenate([rim, values], axis=0).astype(f32)
    conv_acc = conv_w[0] * extended[span:]
    for lag in range(1, span + 1):
        conv_acc = conv_acc + conv_w[lag] * extended[span - lag : span - lag + rows]
    conv_out = conv_acc.astype(bf16)
    query_blocks = to_blocks(query.astype(f32), BLOCK, heads)
    key_blocks = to_blocks(key_feat.astype(f32), BLOCK, heads)
    fq = features(query_blocks, FD).astype(bf16)
    fk = features(key_blocks, FD).astype(bf16)
    vc = to_blocks(conv_out, BLOCK, heads)
    attend = (jnp.einsum("nhif,nhjf->nhij", fq, fk, preferred_element_type=f32) * mask).astype(bf16)
    block_states = jnp.einsum("nhjf,nhjd->nhfd", fk, vc, preferred_element_type=f32)
    own_total = jnp.sum(block_states, axis=0)
    earlier = entering(own_total, "seq", add_states, jnp.zeros_like(own_total))
    previous = (earlier[None] + exclusive_forward(block_states)).astype(bf16)
    hidden = jnp.einsum("nhij,nhjd->nhid", attend, vc, preferred_element_type=f32) + jnp.einsum(
        "nhif,nhfd->nhid", fq, previous, preferred_element_type=f32
    )
    scale = lax.rsqrt(jnp.mean(hidden * hidden, axis=-1, keepdims=True) + EPSILON)
    normed = hidden * scale
    gain_blocks = gain.reshape(heads, 1, gain.shape[0] // heads)
    out_heads = from_blocks((normed * gain_blocks).astype(bf16))
    partial_out = lax.dot_general(
        out_heads, w_out, (((1,), (1,)), ((), ())), preferred_element_type=f32
    )
    mixed = (
        lax.psum_scatter(partial_out.astype(jnp.bfloat16), "head", scatter_dimension=1, tiled=True)
        .astype(jnp.float32)
        .astype(bf16)
    )
    cot_full = lax.all_gather(cotangent, "head", axis=1, tiled=True)
    grad_out = jnp.dot(cot_full, w_out, preferred_element_type=f32)
    grad_w_out = (
        lax.psum_scatter(
            lax.dot_general(
                cot_full, out_heads, (((0,), (0,)), ((), ())), preferred_element_type=f32
            ).astype(jnp.bfloat16),
            "seq",
            scatter_dimension=0,
            tiled=True,
        )
        .astype(jnp.float32)
        .astype(bf16)
    )
    grad_normed = to_blocks(grad_out, BLOCK, heads) * gain_blocks
    grad_hidden = (
        scale * (grad_normed - normed * jnp.mean(grad_normed * normed, axis=-1, keepdims=True))
    ).astype(bf16)
    block_grads = jnp.einsum("nhif,nhid->nhfd", fq, grad_hidden, preferred_element_type=f32)
    own_grad = jnp.sum(block_grads, axis=0)
    later = carried_in(own_grad, "seq", add_states, jnp.zeros_like(own_grad))
    following = (later[None] + exclusive_backward(block_grads)).astype(bf16)
    grad_conv = from_blocks(
        jnp.einsum("nhij,nhid->nhjd", attend, grad_hidden, preferred_element_type=f32)
        + jnp.einsum("nhjf,nhfd->nhjd", fk, following, preferred_element_type=f32)
    )
    products = (
        jnp.einsum("nhid,nhjd->nhij", grad_hidden, vc, preferred_element_type=f32) * mask
    ).astype(bf16)
    grad_fq = jnp.einsum("nhij,nhjf->nhif", products, fk, preferred_element_type=f32) + jnp.einsum(
        "nhid,nhfd->nhif", grad_hidden, previous, preferred_element_type=f32
    )
    grad_fk = jnp.einsum("nhij,nhif->nhjf", products, fq, preferred_element_type=f32) + jnp.einsum(
        "nhjd,nhfd->nhjf", vc, following, preferred_element_type=f32
    )
    grad_query = from_blocks(feature_grad(grad_fq, query_blocks, FD)).astype(bf16)
    grad_key = from_blocks(feature_grad(grad_fk, key_blocks, FD)).astype(bf16)
    leading = grad_conv[:span]
    rim_back = from_behind(leading, "seq", -1)
    grad_extended = jnp.concatenate([grad_conv, rim_back], axis=0)
    grad_acc = conv_w[0] * grad_conv
    for lag in range(1, span + 1):
        grad_acc = grad_acc + conv_w[lag] * grad_extended[lag : lag + rows]
    grad_values = grad_acc.astype(bf16)
    return (mixed, grad_query, grad_key, grad_values, grad_w_out)


def solution(mesh):
    placed = (
        P("seq", "head"),
        P("seq", "head"),
        P("seq", "head"),
        P(None, "head"),
        P("head"),
        P(None, "head"),
        P("seq", "head"),
    )
    return jax.shard_map(
        on_device,
        mesh=mesh,
        in_specs=placed,
        out_specs=(
            P("seq", "head"),
            P("seq", "head"),
            P("seq", "head"),
            P("seq", "head"),
            P("seq", "head"),
        ),
        check_vma=False,
    )
```

profile of v0, /device:TPU:4, one launch (start us, length us, event | category | flops | bytes accessed | tf_op | source)
XLA Modules:
  0.0 450.7 jit_solution(18132834173940098444)
XLA Ops:
  8.0 1.4 slice.55
  9.3 1.9 collective-permute-start
  15.1 1.6 collective-permute-done
  17.6 1.6 fusion.5
  19.3 1.3 reshape.93
  20.6 3.3 fusion.44
  24.0 1.1 bitcast_convert_fusion.1
  25.8 2.6 multiply_convert_fusion.1
  28.4 1.1 fusion.46
  29.5 1.3 slice.74
  30.8 2.2 fusion.19
  33.0 62.4 %all-gather.6.cloned.1.call-done = bf16[1024,4096]{1,0:T(8,128)(2,1)} async-done(((bf16[1024,1024]{1,0:T(8,128)(2,1)}), bf16[1024,4096]{1,0:T(8,128)(2,1)}) %all-gather.6.cloned.1.call-update) | async-done | bytes 8388624 | tf_op jit(solution)/shard_map/all_gather | solution.py:129
  95.4 8.1 %fusion.48 = f32[1024,512]{1,0:T(8,128)S(1)} fusion(bf16[1024,4096]{1,0:T(8,128)(2,1)} %all-gather.6.cloned.1.call-done, bf16[4096,512]{1,0:T(8,128)(2,1)} %param.16), kind=kOutput, calls=%fused_computation.92 | convolution fusion | flops 4294967296 | bytes 14680064 | tf_op jit(solution)/shard_map/dot_general | solution.py:130
  103.5 1.7 reshape.95
  105.2 1.9 copy.40
  107.2 67.9 %all-gather.8.cloned.1.call-done = f32[128,273,128]{2,1,0:T(8,128)} async-done(((f32[4,273,128]{2,1,0:T(8,128)}), f32[128,273,128]{2,1,0:T(8,128)}) %all-gather.8.cloned.1.call-update) | async-done | bytes 17891344 | tf_op jit(solution)/shard_map/all_gather | solution.py:21
  175.1 19.2 %while.22 = (s32[]{:T(128)}, f32[4,273,128]{2,1,0:T(8,128)S(1)}, s32[]{:T(128)}, f32[32,4,273,128]{3,2,1,0:T(8,128)}, s32[]{:T(128)}, /*index=5*/s32[]{:T(128)}, s32[]{:T(128)}) while((s32[]{:T(128)}, f32[4,273,128]{2,1,0:T(8,128)S(1)}, s32[]{:T(128)}, f32[32,4,273,128]{3,2,1,0:T(8,128)}, s32[]{:T(128)}, /*index=5*/s32[]{:T(128)}, ...), condition=%wide.region_2.3_spmd, body=%wide.region_1.2_spmd.sunk | while | flops 139781 | bytes 1677427 | solution.py:27
  175.2 1.2 bitcast_add_fusion.2
  176.4 1.2 bitcast_add_fusion.2
  177.6 1.2 bitcast_add_fusion.2
  178.8 1.2 bitcast_add_fusion.2
  180.0 1.2 bitcast_add_fusion.2
  181.2 1.2 bitcast_add_fusion.2
  182.4 1.2 bitcast_add_fusion.2
  183.6 1.2 bitcast_add_fusion.2
  184.8 1.2 bitcast_add_fusion.2
  186.0 1.2 bitcast_add_fusion.2
  187.2 1.2 bitcast_add_fusion.2
  188.4 1.2 bitcast_add_fusion.2
  189.6 1.2 bitcast_add_fusion.2
  190.8 1.2 bitcast_add_fusion.2
  192.0 1.2 bitcast_add_fusion.2
  193.2 1.2 bitcast_add_fusion.2
  194.4 4.1 multiply_reduce_fusion.4
  200.8 3.1 fusion.45
  204.1 1.9 fusion.11
  206.7 9.6 %fusion = bf16[4096,512]{0,1:T(8,128)(2,1)} fusion(bf16[1024,4096]{1,0:T(8,128)(2,1)} %all-gather.6.cloned.1.call-done, bf16[128,8,4,128]{3,2,1,0:T(4,128)(2,1)S(1)} %bitcast.131), kind=kOutput, calls=%fused_computation.4 | convolution fusion | flops 4297064448 | bytes 13631488 | tf_op jit(solution)/shard_map/dot_general | solution.py:133
  216.3 6.5 %copy.80 = bf16[4096,512]{1,0:T(8,128)(2,1)} copy(bf16[4096,512]{0,1:T(8,128)(2,1)} %fusion) | data formatting | bytes 8388608
  222.9 8.9 %convolution_convert_fusion = bf16[1024,4096]{1,0:T(8,128)(2,1)} fusion(bf16[4096,512]{1,0:T(8,128)(2,1)} %param.16, bf16[128,8,4,128]{3,2,1,0:T(4,128)(2,1)S(1)} %bitcast.132), kind=kOutput, calls=%fused_computation.2 | convolution fusion | flops 4299161600 | bytes 13631488 | tf_op jit(solution)/shard_map/dot_general | solution.py:121
  231.8 1.8 rev.4
  233.6 1.1 fusion.47
  234.9 1.4 slice.65
  236.3 2.5 multiply_convert_fusion
  240.4 1.2 convolution_add_fusion.1
  243.3 1.6 multiply_reduce_fusion.3
  245.8 2.2 fusion.49
  247.9 27.5 %all-gather.10.cloned.1.call-done = bf16[128,273,128]{2,1,0:T(8,128)(2,1)} async-done(((bf16[4,273,128]{2,1,0:T(8,128)(2,1)}), bf16[128,273,128]{2,1,0:T(8,128)(2,1)}) %all-gather.10.cloned.1.call-update) | async-done | bytes 8945680 | tf_op jit(solution)/shard_map/all_gather | solution.py:34
  275.5 16.7 %while.23 = (s32[]{:T(128)}, f32[4,273,128]{2,1,0:T(8,128)S(1)}, s32[]{:T(128)}, bf16[32,4,273,128]{3,2,1,0:T(8,128)(2,1)}, s32[]{:T(128)}, /*index=5*/s32[]{:T(128)}, s32[]{:T(128)}, s32[]{:T(128)}) while((s32[]{:T(128)}, f32[4,273,128]{2,1,0:T(8,128)S(1)}, s32[]{:T(128)}, bf16[32,4,273,128]{3,2,1,0:T(8,128)(2,1)}, s32[]{:T(128)}, ...), condition=%wide.region_9.10_spmd, body=%wide.region_8.9_spmd.sunk | while | flops 279558 | bytes 1397895 | solution.py:41
  275.7 1.1 convert_add_fusion.2
  276.8 1.1 convert_add_fusion.2
  277.9 1.1 convert_add_fusion.2
  286.7 1.1 convert_add_fusion.2
  287.8 1.1 convert_add_fusion.2
  288.9 1.1 convert_add_fusion.2
  290.0 1.1 convert_add_fusion.2
  291.1 1.1 convert_add_fusion.2
  292.2 4.5 add_bitcast_fusion
  296.7 1.4 copy.48
  298.3 4.3 collective-permute-start.1
  303.5 1.1 convolution_add_fusion
  306.0 1.6 multiply_reduce_fusion.1
  308.5 1.6 fusion.2
  310.1 50.5 %reduce-scatter.7.cloned.1.call-done = bf16[128,512]{1,0:T(8,128)(2,1)} async-done(((bf16[4096,512]{1,0:T(8,128)(2,1)}), bf16[128,512]{1,0:T(8,128)(2,1)}) %reduce-scatter.7.cloned.1.call-update) | async-done | bytes 131088
  360.6 83.5 %reduce-scatter.5.cloned.1.call-done = bf16[1024,1024]{1,0:T(8,128)(2,1)} async-done(((bf16[1024,4096]{1,0:T(8,128)(2,1)}), bf16[1024,1024]{1,0:T(8,128)(2,1)}) %reduce-scatter.5.cloned.1.call-update) | async-done | bytes 2097168 | tf_op jit(solution)/shard_map/reduce_scatter | solution.py:125
  (102 shorter events, 24.7 us)
Async XLA Ops:
  7.2 5.1 %copy-start.23 = (bf16[1024,64]{0,1:T(8,128)(2,1)S(1)}, bf16[1024,64]{0,1:T(8,128)(2,1)}, u32[]{:S(2)}) copy-start(bf16[1024,64]{0,1:T(8,128)(2,1)} %param.12) | copy-start | bytes 393220
  7.2 88.2 %all-gather.6.cloned.1.call-start = ((), (), s32[]{:S(2)}) async-start(), calls=%async_computation.3 | async-start | bytes 10485760 | tf_op jit(solution)/shard_map/all_gather | solution.py:129
  7.9 8.7 %copy-start.18 = (bf16[1024,512]{1,0:T(8,128)(2,1)S(1)}, bf16[1024,512]{1,0:T(8,128)(2,1)}, u32[]{:S(2)}) copy-start(bf16[1024,512]{1,0:T(8,128)(2,1)} %param.13) | copy-start | bytes 3145732
  7.9 167.2 %all-gather.8.cloned.1.call-start = ((), (), s32[]{:S(2)}) async-start(), calls=%async_computation.4 | async-start | bytes 18923520 | tf_op jit(solution)/shard_map/all_gather | solution.py:21
  9.3 7.3 %collective-permute-start = (bf16[2,512]{1,0:T(2,128)(2,1)}, bf16[2,512]{1,0:T(2,128)(2,1)}, u32[]{:S(2)}, u32[]{:S(2)}) collective-permute-start(bf16[2,512]{1,0:T(2,128)(2,1)} %slice.55), channel_id=1, source_target_pairs={{0,4},{4,8},{8,12},{12,16},{16,20},{20,24},{24,28},{28,32},{32,36}... | collective-permute-start | bytes 6152 | tf_op jit(solution)/shard_map/ppermute | solution.py:16
  12.2 0.7 copy-start.17
  14.2 11.6 %copy-start = (bf16[4,4,256,16,16]{2,4,3,1,0:T(8,128)(2,1)}, bf16[4,4,256,16,16]{2,4,3,1,0:T(8,128)(2,1)S(1)}, u32[]{:S(2)}) copy-start(bf16[4,4,256,16,16]{2,4,3,1,0:T(8,128)(2,1)S(1)} %multiply_convert_fusion.2) | copy-start | bytes 6291460
  20.6 10.2 %copy-start.5 = (bf16[4,256,4,128]{3,2,1,0:T(4,128)(2,1)}, bf16[4,256,4,128]{3,2,1,0:T(4,128)(2,1)S(1)}, u32[]{:S(2)}) copy-start(bf16[4,256,4,128]{3,2,1,0:T(4,128)(2,1)S(1)} %reshape.93) | copy-start | bytes 3145732
  23.9 251.5 %all-gather.10.cloned.1.call-start = ((), (), s32[]{:S(2)}) async-start(), calls=%async_computation.5 | async-start | bytes 9461760 | tf_op jit(solution)/shard_map/all_gather | solution.py:34
  23.9 1.8 copy-start.21
  24.0 4.4 copy-start.19
  25.1 0.7 copy-start.14
  25.7 2.7 copy-start.8
  25.8 2.6 copy-start.16
  28.4 2.4 copy-start.11
  175.1 19.2 %copy-start.22 = (bf16[4,4,256,16]{2,3,1,0:T(8,128)(2,1)S(1)}, bf16[4,4,256,16]{2,3,1,0:T(8,128)(2,1)}, u32[]{:S(2)}) copy-start(bf16[4,4,256,16]{2,3,1,0:T(8,128)(2,1)} %get-tuple-element.129) | copy-start | bytes 393220
  194.4 4.1 copy-start.24
  198.4 1.3 copy-start.2
  199.0 1.7 copy-start.9
  200.8 3.1 copy-start.3
  203.9 156.7 %reduce-scatter.7.cloned.1.call-start = ((), (), s32[]{:S(2)}) async-start(), calls=%async_computation.6 | async-start | bytes 4325376
  222.8 221.3 %reduce-scatter.5.cloned.1.call-start = ((), (), s32[]{:S(2)}) async-start(), calls=%async_computation.2 | async-start | bytes 10485760 | tf_op jit(solution)/shard_map/reduce_scatter | solution.py:125
  234.9 1.4 copy-start.20
  236.3 2.5 copy-start.4
  236.3 2.5 copy-start.13
  238.8 1.6 copy-start.1
  241.7 1.0 copy-start.15
  243.3 2.5 copy-start.12
  298.1 4.5 %copy-start.6 = (bf16[4,256,4,128]{3,2,1,0:T(4,128)(2,1)S(1)}, bf16[4,256,4,128]{3,2,1,0:T(4,128)(2,1)}, u32[]{:S(2)}) copy-start(bf16[4,256,4,128]{3,2,1,0:T(4,128)(2,1)} %copy-done.5) | copy-start | bytes 3145732
  298.1 4.5 %copy-start.7 = (f32[3,4,273,128]{3,2,1,0:T(8,128)S(1)}, f32[3,4,273,128]{3,2,1,0:T(8,128)}, u32[]{:S(2)}) copy-start(f32[3,4,273,128]{3,2,1,0:T(8,128)} %slice.65) | copy-start | bytes 5031940
  298.3 5.2 %copy-start.10 = (bf16[4,4,256,16,16]{2,4,3,1,0:T(8,128)(2,1)S(1)}, bf16[4,4,256,16,16]{2,4,3,1,0:T(8,128)(2,1)}, u32[]{:S(2)}) copy-start(bf16[4,4,256,16,16]{2,4,3,1,0:T(8,128)(2,1)} %copy-done.8) | copy-start | bytes 6291460
  298.3 10.2 %collective-permute-start.1 = (f32[2,512]{1,0:T(2,128)S(1)}, f32[2,512]{1,0:T(2,128)S(1)}, u32[]{:S(2)}, u32[]{:S(2)}) collective-permute-start(f32[2,512]{1,0:T(2,128)S(1)} %slice.80), channel_id=1, source_target_pairs={{4,0},{8,4},{12,8},{16,12},{20,16},{24,20},{28,24},{32,28},{36,32}... | collective-permute-start | bytes 12296 | tf_op jit(solution)/shard_map/ppermute | solution.py:16
Sparse Core Ops, SparseCore 0:
  9.7 85.6 all-gather.5
  98.2 76.8 all-gather.7
  204.0 71.3 all-gather.9
  279.5 81.0 reduce-scatter.6
  363.7 80.4 reduce-scatter.4
where the time goes:
time: 454 us; the launch traced here: 451 us
  waiting for transfers between devices  294 us (65%)
  matrix products  55 us (12%)
  other arithmetic  53.1 us (12%)
  local copies, waits for them, and re-layouts  26.5 us (6%)
  between operations  14.4 us (3%)
  starting transfers between devices  6.61 us (1%)
    reduce_scatter x1, waiting for transfers between devices, on_device(): lax.psum_scatter(partial_out.astype(jnp.bfloat16), 'head', scatter_dimens...  83.5 us
    all_gather x1, waiting for transfers between devices, entering(): gathered = lax.all_gather(part, axis)  67.9 us
    all_gather x1, waiting for transfers between devices, on_device(): cot_full = lax.all_gather(cotangent, 'head', axis=1, tiled=True)  62.4 us
    unnamed x6, waiting for transfers between devices  51.3 us
    add x31, other arithmetic, add_states(): return earlier + later  34.9 us
    all_gather x1, waiting for transfers between devices, carried_in(): gathered = lax.all_gather(x.astype(jnp.bfloat16), axis)  27.5 us
    unnamed x55, local copies, waits for them, and re-layouts  11.3 us
    dot_general x1, matrix products, on_device(): lax.dot_general(cot_full, out_heads, (((0,), (0,)), ((), ())), preferred_...  9.62 us
  transfers between devices with their start and end apart: 7, of which 6 were waited for; matrix products, arithmetic and copies ran while one was open for 23% of the time, Pallas kernels for 0%

commit v1 on v0

v1 whole, which is shorter than its diff:
```python
import functools

import jax
import jax.numpy as jnp
from jax import lax
from jax.experimental import pallas as pl
from jax.experimental.pallas import tpu as pltpu
from jax.sharding import PartitionSpec as P

f32 = jnp.float32
bf16 = jnp.bfloat16
FD = 16
BLOCK = 256
ROWS = 1024
HEADS = 4
NB = ROWS // BLOCK
DV = 128
CH = HEADS * DV
FEAT = 1024
NF = 160
EPSILON = 1e-05
VMEM_LIMIT = 56 * 1024 * 1024


def nn(a, b):
    return lax.dot_general(a, b, (((1,), (0,)), ((), ())), preferred_element_type=f32)


def nt(a, b):
    return lax.dot_general(a, b, (((1,), (1,)), ((), ())), preferred_element_type=f32)


def tn(a, b):
    return lax.dot_general(a, b, (((0,), (0,)), ((), ())), preferred_element_type=f32)


def place():
    s = lax.axis_index("seq")
    z = lax.axis_index("head")
    return s, z, s // 8, (s // 2) % 4, s % 2


def seq_of(x, y, c):
    return (x * 4 + y) * 2 + c


def remote(src, dst, send_sem, recv_sem, seq, head):
    copy = pltpu.make_async_remote_copy(
        src_ref=src,
        dst_ref=dst,
        send_sem=send_sem,
        recv_sem=recv_sem,
        device_id={"seq": seq, "head": head},
        device_id_type=pl.DeviceIdType.MESH,
    )
    copy.start()
    return copy


def greet(devices):
    barrier = pltpu.get_barrier_semaphore()
    for seq, head in devices:
        pl.semaphore_signal(
            barrier, inc=1, device_id={"seq": seq, "head": head}, device_id_type=pl.DeviceIdType.MESH
        )
    pl.semaphore_wait(barrier, len(devices))


def plane_peers(s, z, x, y, c):
    out = [(seq_of(x, y, 1 - c), z)]
    for j in (1, 2, 3):
        out.append((seq_of((x + j) % 4, y, c), z))
        out.append((seq_of(x, (y + j) % 4, c), z))
    return out


def eye64():
    r = lax.broadcasted_iota(jnp.int32, (64, 64), 0)
    c = lax.broadcasted_iota(jnp.int32, (64, 64), 1)
    return (r == c).astype(bf16)


def spread(x_ref, x2_ref):
    xt = nt(eye64(), x_ref[...])
    for h in range(HEADS):
        x2_ref[h, 0:16, :] = xt[16 * h : 16 * h + 16]
        x2_ref[h, 16:32, :] = xt[16 * h : 16 * h + 16]


def phi(x2_ref, h, cols):
    x = x2_ref[h, 0:16, cols]
    parts = [x * x]
    for d in range(1, 8):
        parts.append(x * x2_ref[h, d : d + 16, cols])
    parts.append(x[0:8] * x2_ref[h, 8:16, cols])
    parts.append((lax.broadcasted_iota(jnp.int32, (8, BLOCK), 0) == 0).astype(f32))
    parts.append(x)
    return jnp.concatenate(parts, axis=0).astype(bf16)


def phi_back(g, x2_ref, t2_ref, h, cols):
    x = x2_ref[h, 0:16, cols]
    acc = g[144:160] + 2.0 * g[0:16] * x
    for d in range(1, 8):
        gd = g[16 * d : 16 * d + 16]
        acc = acc + gd * x2_ref[h, d : d + 16, cols]
        t = gd * x
        t2_ref[d - 1, 0:16, :] = t
        t2_ref[d - 1, 16:32, :] = t
        acc = acc + t2_ref[d - 1, 16 - d : 32 - d, :]
    g8 = g[128:136]
    low = g8 * x2_ref[h, 8:16, cols]
    high = g8 * x[0:8]
    return acc + jnp.concatenate([low, high], axis=0)


def weights():
    r = lax.broadcasted_iota(jnp.int32, (NF, DV), 0)
    return jnp.where(
        r < 16, 1.0 / 32, jnp.where(r < 136, 1.0 / 16, jnp.where(r < 144, 1.0, 0.25))
    ).astype(f32)


def head_lanes(h):
    lane = lax.broadcasted_iota(jnp.int32, (BLOCK, HEADS * FD), 1)
    return (lane >= 16 * h) & (lane < 16 * h + 16)


def lower():
    r = lax.broadcasted_iota(jnp.int32, (BLOCK, BLOCK), 0)
    c = lax.broadcasted_iota(jnp.int32, (BLOCK, BLOCK), 1)
    return r >= c


def only(x, mask):
    return jnp.where(mask, x.astype(f32), 0.0).astype(bf16)


SCAN_SCRATCH = [
    pltpu.VMEM((HEADS, NF, DV), f32),
    pltpu.VMEM((2, NF, DV), f32),
    pltpu.VMEM((2, NF, DV), bf16),
    pltpu.VMEM((3, 2, NF, DV), bf16),
    pltpu.VMEM((2, NF, DV), bf16),
    pltpu.VMEM((3, 2, NF, DV), bf16),
    pltpu.VMEM((2, NF, DV), f32),
    pltpu.VMEM((2, NF, DV), f32),
    pltpu.VMEM((2, NF, DV), f32),
    pltpu.VMEM((HEADS, NF, DV), f32),
    pltpu.SemaphoreType.DMA((8,)),
    pltpu.SemaphoreType.DMA((8,)),
]


def scan_steps(refs, forward):
    tot, ra, ys, yr, xs, xr, py, fs, fr, ent, ssem, rsem = refs
    s, z, x, y, c = place()
    sibling = seq_of(x, y, 1 - c)
    mine = pl.ds(2 * c, 2)
    copies = {}

    def counts(me, j):
        met = (me - j >= 0) if forward else (me - j < 0)
        return jnp.where(met, 1.0, 0.0).astype(f32)

    def pair():
        copies["a"] = remote(tot.at[pl.ds(2 * (1 - c), 2)], ra, ssem.at[0], rsem.at[0], sibling, z)

    def along_y():
        copies["a"].wait_recv()
        ys[...] = (tot[mine] + ra[...]).astype(bf16)
        for j in (1, 2, 3):
            copies["y", j] = remote(
                ys, yr.at[j - 1], ssem.at[j], rsem.at[j], seq_of(x, (y + j) % 4, c), z
            )

    def along_x():
        row = tot[mine] + ra[...]
        before = jnp.zeros((2, NF, DV), f32)
        for j in (1, 3, 2):
            copies["y", j].wait_recv()
            got = yr[j - 1].astype(f32)
            row = row + got
            before = before + got * counts(y, j)
        xs[...] = row.astype(bf16)
        py[...] = before
        for j in (1, 2, 3):
            copies["x", j] = remote(
                xs, xr.at[j - 1], ssem.at[3 + j], rsem.at[3 + j], seq_of((x + j) % 4, y, c), z
            )

    def back():
        before = py[...]
        for j in (1, 3, 2):
            copies["x", j].wait_recv()
            before = before + xr[j - 1].astype(f32) * counts(x, j)
        first = jnp.where(c == 0, 1.0, 0.0).astype(f32)
        other = first if forward else 1.0 - first
        fs[...] = before + tot[mine] * other
        ent[mine] = before + ra[...] * (1.0 - other)
        copies["f"] = remote(fs, fr, ssem.at[7], rsem.at[7], sibling, z)

    def done():
        copies["f"].wait_recv()
        ent[pl.ds(2 * (1 - c), 2)] = fr[...]
        for copy in copies.values():
            copy.wait_send()

    return pair, along_y, along_x, back, done


def forward_kernel(
    q_ref, k_ref, v_ref, cw_ref, gain_ref,
    o_ref, hid_ref, conv_ref, prev_ref,
    halo, vx, qx, kx, st, hsem, *scan_refs,
):
    s, z, x, y, c = place()
    tot, ent = scan_refs[0], scan_refs[9]
    after, before = (s + 1) % 32, (s + 31) % 32
    greet(plane_peers(s, z, x, y, c) + [(after, z), (before, z)])
    edge = remote(v_ref.at[pl.ds(ROWS - 16, 16)], halo, hsem.at[0], hsem.at[1], after, z)
    spread(k_ref, kx)
    spread(q_ref, qx)
    vx[8 : 8 + ROWS, :] = v_ref[...].astype(f32)
    edge.wait_recv()
    inside = jnp.where(s > 0, 1.0, 0.0).astype(f32)
    vx[0:8, :] = halo[...].astype(f32)[8:16] * inside
    for n in range(NB):
        at = 8 + n * BLOCK
        acc = cw_ref[0:1, :] * vx[at : at + BLOCK, :]
        for j in (1, 2):
            acc = acc + cw_ref[j : j + 1, :] * vx[at - j : at - j + BLOCK, :]
        conv_ref[n * BLOCK : (n + 1) * BLOCK, :] = acc.astype(bf16)
    tot[...] = jnp.zeros_like(tot)

    def states(n, carry):
        rows = pl.ds(pl.multiple_of(n * BLOCK, BLOCK), BLOCK)
        for h in range(HEADS):
            own = nn(phi(kx, h, rows), conv_ref[rows, h * DV : (h + 1) * DV])
            st[n, h] = own
            tot[h] += own
        return carry

    lax.fori_loop(0, NB, states, 0)
    pair, along_y, along_x, back, done = scan_steps(scan_refs, True)
    mask = lower()

    def intra(n, carry):
        rows = pl.ds(pl.multiple_of(n * BLOCK, BLOCK), BLOCK)
        q = q_ref[rows, :]
        k = k_ref[rows, :]
        for h in range(HEADS):
            sc = nt(q, only(k, head_lanes(h)))
            att = jnp.where(mask, 1.0 + sc * (0.25 + sc * (1.0 / 32)), 0.0).astype(bf16)
            hid_ref[rows, h * DV : (h + 1) * DV] = nn(att, conv_ref[rows, h * DV : (h + 1) * DV])
        return carry

    pair()
    lax.fori_loop(0, 1, intra, 0)
    along_y()
    lax.fori_loop(1, 3, intra, 0)
    along_x()
    lax.fori_loop(3, 4, intra, 0)
    back()
    done()
    wts = weights()

    def finish(n, carry):
        rows = pl.ds(pl.multiple_of(n * BLOCK, BLOCK), BLOCK)
        for h in range(HEADS):
            lanes = slice(h * DV, (h + 1) * DV)
            state = ent[h]
            ent[h] = state + st[n, h]
            prev = (state * wts).astype(bf16)
            prev_ref[n, h] = prev
            hidden = hid_ref[rows, lanes] + tn(phi(qx, h, rows), prev)
            hid_ref[rows, lanes] = hidden
            scale = lax.rsqrt(jnp.mean(hidden * hidden, axis=-1, keepdims=True) + EPSILON)
            o_ref[rows, lanes] = (hidden * scale * gain_ref[0:1, lanes]).astype(bf16)
        return carry

    lax.fori_loop(0, NB, finish, 0)
    edge.wait_send()


def forward_call(q, k, v, cw, gain):
    vm = pl.BlockSpec(memory_space=pltpu.VMEM)
    return pl.pallas_call(
        forward_kernel,
        out_shape=(
            jax.ShapeDtypeStruct((ROWS, CH), bf16),
            jax.ShapeDtypeStruct((ROWS, CH), f32),
            jax.ShapeDtypeStruct((ROWS, CH), bf16),
            jax.ShapeDtypeStruct((NB, HEADS, NF, DV), bf16),
        ),
        in_specs=[vm] * 5,
        out_specs=(vm,) * 4,
        scratch_shapes=[
            pltpu.VMEM((16, CH), bf16),
            pltpu.VMEM((8 + ROWS, CH), f32),
            pltpu.VMEM((HEADS, 32, ROWS), f32),
            pltpu.VMEM((HEADS, 32, ROWS), f32),
            pltpu.VMEM((NB, HEADS, NF, DV), f32),
            pltpu.SemaphoreType.DMA((2,)),
        ]
        + SCAN_SCRATCH,
        compiler_params=pltpu.CompilerParams(
            collective_id=0, has_side_effects=True, vmem_limit_bytes=VMEM_LIMIT
        ),
        name="forward_attention",
    )(q, k, v, cw, gain)


def project_kernel(
    o_hbm, w_hbm, cot_hbm,
    mixed_ref, gw_ref, go_ref,
    oall, wt, cot, cott, opp, to_r, to_l, opp_l, opp_r, from_r, from_l,
    gwp, r1, gsum, yr, xs, xr, fin, lsem, zs, zr, ws, wr, gs, gr,
):
    s, z, x, y, c = place()
    right, left = (z + 1) % 4, (z + 3) % 4
    sibling = seq_of(x, y, 1 - c)
    partner = (seq_of(z, y, c), x)
    greet(
        plane_peers(s, z, x, y, c)
        + [(s, (z + k) % 4) for k in (1, 2, 3)]
        + [partner]
    )
    sends = []

    def go(*args):
        copy = remote(*args)
        sends.append(copy)
        return copy

    ag = {}
    for b in (0, 1, 2, 3):
        to_right = pl.ds(b * BLOCK, BLOCK)
        ag["l", b] = go(o_hbm.at[to_right], oall.at[3, to_right], zs.at[b], zr.at[b], s, right)
        e = (b + 2) % 4
        to_left = pl.ds(e * BLOCK, BLOCK)
        ag["r", e] = go(
            o_hbm.at[to_left], oall.at[1, to_left], zs.at[4 + e], zr.at[4 + e], s, left
        )
    row = c * 512 + x * 128 + y * 32
    wz = {}
    for k in (1, 2, 3):
        there = (z + k) % 4
        wz[k] = go(
            w_hbm.at[pl.ds(pl.multiple_of(there * FEAT + row, 32), 32)],
            wt.at[4 - k, pl.ds(pl.multiple_of(row, 32), 32)],
            ws.at[k - 1],
            wr.at[k - 1],
            s,
            there,
        )
    load_cot = pltpu.make_async_copy(cot_hbm, cot, lsem.at[0])
    load_cot.start()
    load_w = pltpu.make_async_copy(
        w_hbm.at[pl.ds(pl.multiple_of(z * FEAT, FEAT), FEAT)], wt.at[0], lsem.at[1]
    )
    load_w.start()
    load_o = pltpu.make_async_copy(o_hbm, oall.at[0], lsem.at[2])
    load_o.start()

    def piece(px, py, half):
        at = pl.multiple_of(c * 512 + px * 128 + py * 32, 32)
        return wt.at[pl.ds(1, 3), pl.ds(at, 32), pl.ds(half * 256, 256)]

    for k in (1, 2, 3):
        wz[k].wait_recv()
    w1 = {}
    for j in (1, 2, 3):
        own = piece(x, y, 0)
        w1[0, j] = go(own, own, ws.at[2 + j], wr.at[2 + j], seq_of((x + j) % 4, y, c), z)
        own = piece(x, y, 1)
        w1[1, j] = go(own, own, ws.at[5 + j], wr.at[5 + j], seq_of(x, (y + j) % 4, c), z)

    load_cot.wait()

    def flip(b, carry):
        at = pl.ds(pl.multiple_of(b * BLOCK, BLOCK), BLOCK)
        cott[:, at] = jnp.transpose(cot[at, :], (1, 0))
        return carry

    lax.fori_loop(0, NB, flip, 0)

    w2 = {}
    index = 9
    for i in (0, 1, 3, 2):
        for half in (0, 1):
            if i:
                w1[half, i].wait_recv()
            block = piece((x - i + 4) % 4, y, 0) if half == 0 else piece(x, (y - i + 4) % 4, 1)
            for j in (1, 2, 3):
                to = seq_of(x, (y + j) % 4, c) if half == 0 else seq_of((x + j) % 4, y, c)
                w2[half, i, j] = go(block, block, ws.at[index], wr.at[index], to, z)
                index += 1

    def gw_term(k):
        group = (z + k) % 4

        def part(t, carry):
            rows = pl.ds(pl.multiple_of(t * 256, 256), 256)
            term = nn(cott[rows, :], oall[k]).astype(bf16)
            gwp[0, group, t] = term[0:128]
            gwp[1, group, t] = term[128:256]
            return carry

        lax.fori_loop(0, 4, part, 0)
        return go(gwp.at[1 - c, group], r1.at[group], gs.at[k], gr.at[k], sibling, z)

    gy = {}

    def gw_pair(k, copy):
        group = (z + k) % 4
        copy.wait_recv()

        def part(t, carry):
            gsum[group, t] = (gwp[c, group, t].astype(f32) + r1[group, t].astype(f32)).astype(bf16)
            return carry

        lax.fori_loop(0, 4, part, 0)
        for j in (1, 2, 3):
            there = (y + j) % 4
            at = 4 + 3 * k + j - 1
            gy[k, j] = go(
                gsum.at[group, there], yr.at[group, j - 1], gs.at[at], gr.at[at], seq_of(x, there, c), z
            )

    def gw_rows(k):
        group = (z + k) % 4
        acc = gsum[group, y].astype(f32)
        for j in (1, 2, 3):
            gy[k, j].wait_recv()
            acc = acc + yr[group, j - 1].astype(f32)
        xs[group] = acc.astype(bf16)

    load_o.wait()
    gw0 = gw_term(0)
    for copy in w2.values():
        copy.wait_recv()
    half_w = wt.at[pl.ds(1, 3), pl.ds(pl.multiple_of(c * 512, 512), 512)]
    w3 = go(half_w, half_w, ws.at[index], wr.at[index], sibling, z)
    gw_pair(0, gw0)

    for b in (0, 1):
        ag["l", b].wait_recv()
        block = pl.ds(b * BLOCK, BLOCK)
        ag["f", b] = go(oall.at[3, block], oall.at[2, block], zs.at[8 + b], zr.at[8 + b], s, right)
        e = b + 2
        ag["r", e].wait_recv()
        block = pl.ds(e * BLOCK, BLOCK)
        ag["f", e] = go(oall.at[1, block], oall.at[2, block], zs.at[8 + e], zr.at[8 + e], s, left)
    w3.wait_recv()
    load_w.wait()

    def go_term(k, b):
        return nn(cot[b * BLOCK : (b + 1) * BLOCK, :], wt[k])

    rs = {}

    def rows_of(b):
        return pl.ds(b * BLOCK, BLOCK)

    def fill(k, dst, lo, hi):
        def part(b, carry):
            rows = pl.ds(pl.multiple_of(b * BLOCK, BLOCK), BLOCK)
            dst[rows, :] = nn(cot[rows, :], wt[k]).astype(bf16)
            return carry

        lax.fori_loop(lo, hi, part, 0)

    half_a, half_b = pl.ds(0, 512), pl.ds(512, 512)
    fill(2, opp, 0, 4)
    rs["or"] = go(opp.at[half_a], opp_l, zs.at[12], zr.at[12], s, right)
    rs["ol"] = go(opp.at[half_b], opp_r, zs.at[13], zr.at[13], s, left)
    fill(1, to_r, 2, 4)
    rs["dr"] = go(to_r.at[half_b], from_l.at[half_b], zs.at[14], zr.at[14], s, right)
    fill(3, to_l, 0, 2)
    rs["dl"] = go(to_l.at[half_a], from_r.at[half_a], zs.at[15], zr.at[15], s, left)

    for b in (2, 3):
        ag["l", b].wait_recv()
        ag["r", b - 2].wait_recv()
    gw1 = gw_term(1)
    gw3 = gw_term(3)
    gw_rows(0)
    gw_pair(1, gw1)
    gw_pair(3, gw3)
    for b in (0, 1, 2, 3):
        ag["f", b].wait_recv()
    gw2 = gw_term(2)

    def mix(t, carry):
        rows = pl.ds(pl.multiple_of((t // 2) * BLOCK, BLOCK), BLOCK)
        for u in (0, 1):
            cols = slice(512 * u, 512 * u + 512)
            acc = nt(oall[0, rows, :], wt[0, cols, :])
            for k in (1, 2, 3):
                acc = acc + nt(oall[k, rows, :], wt[k, cols, :])
            mixed_ref[rows, cols] = acc.astype(bf16)
        return carry

    gw_rows(1)
    gw_rows(3)
    gw_pair(2, gw2)

    def add_in(k, dst, got, lo):
        def part(b, carry):
            rows = pl.ds(pl.multiple_of(lo + b * BLOCK, BLOCK), BLOCK)
            here = pl.ds(pl.multiple_of(b * BLOCK, BLOCK), BLOCK)
            dst[rows, :] = (nn(cot[rows, :], wt[k]) + got[here, :].astype(f32)).astype(bf16)
            return carry

        lax.fori_loop(0, 2, part, 0)

    rs["or"].wait_recv()
    add_in(1, to_r, opp_l, 0)
    rs["ar"] = go(to_r.at[half_a], from_l.at[half_a], zs.at[16], zr.at[16], s, right)
    rs["ol"].wait_recv()
    add_in(3, to_l, opp_r, 512)
    rs["al"] = go(to_l.at[half_b], from_r.at[half_b], zs.at[17], zr.at[17], s, left)

    gw_rows(2)
    gx = {}
    for j in (1, 2, 3):
        there = (x + j) % 4
        gx[j] = go(
            xs.at[there], xr.at[j - 1], gs.at[15 + j], gr.at[15 + j], seq_of(there, y, c), z
        )

    def mix_rows(t, carry):
        return mix(2 * t, carry)

    lax.fori_loop(0, NB, mix_rows, 0)

    total = xs[x].astype(f32)
    for j in (1, 2, 3):
        gx[j].wait_recv()
        total = total + xr[j - 1].astype(f32)
    fin[...] = total.astype(bf16)
    stays = x == z

    @pl.when(stays)
    def _():
        gw_ref[...] = fin[...]

    @pl.when(jnp.logical_not(stays))
    def _():
        move = remote(fin, gw_ref, gs.at[19], gr.at[19], partner[0], partner[1])
        move.wait()

    def own(b, carry):
        rows = pl.ds(pl.multiple_of(b * BLOCK, BLOCK), BLOCK)
        go_ref[rows, :] = nn(cot[rows, :], wt[0])
        return carry

    lax.fori_loop(0, NB, own, 0)
    for name in ("dr", "dl", "ar", "al"):
        rs[name].wait_recv()

    def gather(b, carry):
        rows = pl.ds(pl.multiple_of(b * BLOCK, BLOCK), BLOCK)
        go_ref[rows, :] += from_r[rows, :].astype(f32) + from_l[rows, :].astype(f32)
        return carry

    lax.fori_loop(0, NB, gather, 0)
    for copy in sends:
        copy.wait_send()


def project_call(o, w, cot):
    vm = pl.BlockSpec(memory_space=pltpu.VMEM)
    hbm = pl.BlockSpec(memory_space=pl.ANY)
    dma = pltpu.SemaphoreType.DMA
    return pl.pallas_call(
        project_kernel,
        out_shape=(
            jax.ShapeDtypeStruct((ROWS, FEAT), bf16),
            jax.ShapeDtypeStruct((128, CH), bf16),
            jax.ShapeDtypeStruct((ROWS, CH), f32),
        ),
        in_specs=[hbm] * 3,
        out_specs=(vm,) * 3,
        scratch_shapes=[
            pltpu.VMEM((4, ROWS, CH), bf16),
            pltpu.VMEM((4, FEAT, CH), bf16),
            pltpu.VMEM((ROWS, FEAT), bf16),
            pltpu.VMEM((FEAT, ROWS), bf16),
            pltpu.VMEM((ROWS, CH), bf16),
            pltpu.VMEM((ROWS, CH), bf16),
            pltpu.VMEM((ROWS, CH), bf16),
            pltpu.VMEM((512, CH), bf16),
            pltpu.VMEM((512, CH), bf16),
            pltpu.VMEM((ROWS, CH), bf16),
            pltpu.VMEM((ROWS, CH), bf16),
            pltpu.VMEM((2, 4, 4, 128, CH), bf16),
            pltpu.VMEM((4, 4, 128, CH), bf16),
            pltpu.VMEM((4, 4, 128, CH), bf16),
            pltpu.VMEM((4, 3, 128, CH), bf16),
            pltpu.VMEM((4, 128, CH), bf16),
            pltpu.VMEM((3, 128, CH), bf16),
            pltpu.VMEM((128, CH), bf16),
            dma((3,)),
            dma((18,)),
            dma((18,)),
            dma((34,)),
            dma((34,)),
            dma((20,)),
            dma((20,)),
        ],
        compiler_params=pltpu.CompilerParams(
            collective_id=1, has_side_effects=True, vmem_limit_bytes=VMEM_LIMIT
        ),
        name="projections",
    )(o, w, cot)


def backward_kernel(
    q_ref, k_ref, conv_ref, cw_ref, gain_ref, hid_ref, go_ref, prev_ref,
    gq_ref, gk_ref, gv_ref,
    halo, edge_rows, qx, kx, t2, gh, bg, fw, gc, gi, dx, hsem, *scan_refs,
):
    s, z, x, y, c = place()
    tot, ent = scan_refs[0], scan_refs[9]
    after, before = (s + 1) % 32, (s + 31) % 32
    greet(plane_peers(s, z, x, y, c) + [(after, z), (before, z)])
    spread(k_ref, kx)
    spread(q_ref, qx)
    tot[...] = jnp.zeros_like(tot)

    def states(n, carry):
        rows = pl.ds(pl.multiple_of(n * BLOCK, BLOCK), BLOCK)
        for h in range(HEADS):
            lanes = slice(h * DV, (h + 1) * DV)
            hidden = hid_ref[rows, lanes]
            scale = lax.rsqrt(jnp.mean(hidden * hidden, axis=-1, keepdims=True) + EPSILON)
            normed = hidden * scale
            up = go_ref[rows, lanes] * gain_ref[0:1, lanes]
            grad = scale * (up - normed * jnp.mean(up * normed, axis=-1, keepdims=True))
            grad = grad.astype(bf16)
            gh[rows, lanes] = grad
            own = nn(phi(qx, h, rows), grad)
            bg[n, h] = own
            tot[h] += own
        return carry

    lax.fori_loop(0, NB, states, 0)
    pair, along_y, along_x, back, done = scan_steps(scan_refs, False)
    mask = lower()
    mask_t = jnp.logical_not(mask) | (
        lax.broadcasted_iota(jnp.int32, (BLOCK, BLOCK), 0)
        == lax.broadcasted_iota(jnp.int32, (BLOCK, BLOCK), 1)
    )

    def intra(n, carry):
        rows = pl.ds(pl.multiple_of(n * BLOCK, BLOCK), BLOCK)
        q = q_ref[rows, :]
        k = k_ref[rows, :]
        to_q = jnp.zeros((BLOCK, HEADS * FD), f32)
        to_k = jnp.zeros((BLOCK, HEADS * FD), f32)
        for h in range(HEADS):
            lanes = slice(h * DV, (h + 1) * DV)
            kh = only(k, head_lanes(h))
            qh = only(q, head_lanes(h))
            g = gh[rows, lanes]
            v = conv_ref[rows, lanes]
            sc = nt(qh, kh)
            ds = jnp.where(mask, nt(g, v) * (0.25 + sc * (1.0 / 16)), 0.0).astype(bf16)
            to_q = to_q + nn(ds, kh)
            sc_t = nt(kh, qh)
            ds_t = jnp.where(mask_t, nt(v, g) * (0.25 + sc_t * (1.0 / 16)), 0.0).astype(bf16)
            to_k = to_k + nn(ds_t, qh)
            att = jnp.where(mask_t, 1.0 + sc_t * (0.25 + sc_t * (1.0 / 32)), 0.0).astype(bf16)
            gc[rows, lanes] = nn(att, g)
            dx[16 * h : 16 * h + 16, rows] = phi_back(nt(prev_ref[n, h], g), qx, t2, h, rows)
        gi[rows, 0:64] = to_q
        gi[rows, 64:128] = to_k
        return carry

    pair()
    lax.fori_loop(0, 1, intra, 0)
    along_y()
    lax.fori_loop(1, 3, intra, 0)
    along_x()
    lax.fori_loop(3, 4, intra, 0)
    back()
    done()
    wts = weights()

    def suffix(t, carry):
        n = NB - 1 - t
        for h in range(HEADS):
            state = ent[h]
            ent[h] = state + bg[n, h]
            fw[n, h] = (state * wts).astype(bf16)
        return carry

    lax.fori_loop(0, NB, suffix, 0)

    def finish(n, carry):
        rows = pl.ds(pl.multiple_of(n * BLOCK, BLOCK), BLOCK)
        for h in range(HEADS):
            lanes = slice(h * DV, (h + 1) * DV)
            gc[rows, lanes] += tn(phi(kx, h, rows), fw[n, h])
            grad = nt(fw[n, h], conv_ref[rows, lanes])
            dx[64 + 16 * h : 64 + 16 * h + 16, rows] = phi_back(grad, kx, t2, h, rows)
        both = gi[rows, :] + jnp.transpose(dx[:, rows], (1, 0))
        gq_ref[rows, :] = both[:, 0:64].astype(bf16)
        gk_ref[rows, :] = both[:, 64:128].astype(bf16)
        return carry

    lax.fori_loop(0, 1, finish, 0)
    edge_rows[...] = gc[0:8, :]
    edge = remote(edge_rows, halo, hsem.at[0], hsem.at[1], before, z)
    lax.fori_loop(1, NB, finish, 0)
    edge.wait()
    inside = jnp.where(s < 31, 1.0, 0.0).astype(f32)
    gc[ROWS : ROWS + 8, :] = halo[...] * inside
    for n in range(NB):
        at = n * BLOCK
        acc = cw_ref[0:1, :] * gc[at : at + BLOCK, :]
        for j in (1, 2):
            acc = acc + cw_ref[j : j + 1, :] * gc[at + j : at + j + BLOCK, :]
        gv_ref[at : at + BLOCK, :] = acc.astype(bf16)


def backward_call(q, k, conv, cw, gain, hid, go, prev):
    vm = pl.BlockSpec(memory_space=pltpu.VMEM)
    return pl.pallas_call(
        backward_kernel,
        out_shape=(
            jax.ShapeDtypeStruct((ROWS, HEADS * FD), bf16),
            jax.ShapeDtypeStruct((ROWS, HEADS * FD), bf16),
            jax.ShapeDtypeStruct((ROWS, CH), bf16),
        ),
        in_specs=[vm] * 8,
        out_specs=(vm,) * 3,
        scratch_shapes=[
            pltpu.VMEM((8, CH), f32),
            pltpu.VMEM((8, CH), f32),
            pltpu.VMEM((HEADS, 32, ROWS), f32),
            pltpu.VMEM((HEADS, 32, ROWS), f32),
            pltpu.VMEM((7, 32, BLOCK), f32),
            pltpu.VMEM((ROWS, CH), bf16),
            pltpu.VMEM((NB, HEADS, NF, DV), f32),
            pltpu.VMEM((NB, HEADS, NF, DV), bf16),
            pltpu.VMEM((ROWS + 8, CH), f32),
            pltpu.VMEM((ROWS, 128), f32),
            pltpu.VMEM((128, ROWS), f32),
            pltpu.SemaphoreType.DMA((2,)),
        ]
        + SCAN_SCRATCH,
        compiler_params=pltpu.CompilerParams(
            collective_id=2, has_side_effects=True, vmem_limit_bytes=VMEM_LIMIT
        ),
        name="backward_attention",
    )(q, k, conv, cw, gain, hid, go, prev)


def on_device(query, key_feat, values, conv_w, gain, w_out, cotangent):
    gain = gain.reshape(1, CH)
    heads_out, hidden, conv, prev = forward_call(query, key_feat, values, conv_w, gain)
    mixed, grad_w, grad_out = project_call(heads_out, w_out, cotangent)
    grad_q, grad_k, grad_v = backward_call(
        query, key_feat, conv, conv_w, gain, hidden, grad_out, prev
    )
    return mixed, grad_q, grad_k, grad_v, grad_w


def solution(mesh):
    both = P("seq", "head")
    return jax.shard_map(
        on_device,
        mesh=mesh,
        in_specs=(both, both, both, P(None, "head"), P("head"), P(None, "head"), both),
        out_specs=(both,) * 5,
        check_vma=False,
    )
```

time: 454 us -> 169 us (0.37)
  the two profiles are of different devices: /device:TPU:4 before, /device:TPU:1 now
where the time goes in v1:
time: 169 us
  Pallas kernels  158 us (93%)
  local copies, waits for them, and re-layouts  10.6 us (6%)
    pallas_call x1, Pallas kernels, project_call(): pl.pallas_call(project_kernel, out_shape=(jax.ShapeDtypeStruct((ROWS, FEA...  94.2 us
    pallas_call x1, Pallas kernels, backward_call(): pl.pallas_call(backward_kernel, out_shape=(jax.ShapeDtypeStruct((ROWS, HE...  33.5 us
    pallas_call x1, Pallas kernels, forward_call(): pl.pallas_call(forward_kernel, out_shape=(jax.ShapeDtypeStruct((ROWS, CH)...  29.9 us
    unnamed x13, local copies, waits for them, and re-layouts  10.6 us

profile of v1, /device:TPU:1, one launch (start us, length us, event | category | flops | bytes accessed | tf_op | source)
XLA Modules:
  0.0 168.8 jit_solution(17565846799040271473)
XLA Ops:
  0.6 1.7 %copy.12.q_ref = bf16[1024,64]{1,0:T(8,128)(2,1)} copy(bf16[1024,64]{0,1:T(8,128)(2,1)} %param.7) | data formatting | bytes 262144 | tf_op args[0]
  2.4 1.7 %copy.13.k_ref = bf16[1024,64]{1,0:T(8,128)(2,1)} copy(bf16[1024,64]{0,1:T(8,128)(2,1)} %param.8) | data formatting | bytes 262144 | tf_op args[1]
  4.1 29.9 %forward_attention.1 = (bf16[1024,512]{1,0:T(8,128)(2,1)}, f32[1024,512]{1,0:T(8,128)}, bf16[1024,512]{1,0:T(8,128)(2,1)}, bf16[4,4,160,128]{3,2,1,0:T(8,128)(2,1)}) custom-call(bf16[1024,64]{1,0:T(8,128)(2,1)} %copy.12.q_ref, bf16[1024,64]{1,0:T(8,128)(2,1)} %copy.13.k_ref, bf16[1024,512]{1,0:T(8,128)(2,1)} %v_ref.1, f32[3,512]{1,0:T(4,128)} %cw_ref.3, ...), custom_call_target="tpu_custom_call" | custom-call | tf_op jit(solution)/shard_map/forward_attention/pallas_call | solution.py:288
  34.0 94.2 %projections.1 = (bf16[1024,1024]{1,0:T(8,128)(2,1)}, bf16[128,512]{1,0:T(8,128)(2,1)}, f32[1024,512]{1,0:T(8,128)}) custom-call(bf16[1024,512]{1,0:T(8,128)(2,1)} %get-tuple-element.15.o_hbm, bf16[4096,512]{1,0:T(8,128)(2,1)} %w_hbm.1, bf16[1024,1024]{1,0:T(8,128)(2,1)} %cot_hbm.1), custom_call_target="tpu_custom_call" | custom-call | tf_op jit(solution)/shard_map/projections/pallas_call | solution.py:577
  128.2 0.0 copy-start
  128.2 33.5 %backward_attention.1 = (bf16[1024,64]{1,0:T(8,128)(2,1)}, bf16[1024,64]{1,0:T(8,128)(2,1)}, bf16[1024,512]{1,0:T(8,128)(2,1)}) custom-call(bf16[1024,64]{1,0:T(8,128)(2,1)} %copy.12.q_ref, bf16[1024,64]{1,0:T(8,128)(2,1)} %copy.13.k_ref, bf16[1024,512]{1,0:T(8,128)(2,1)} %get-tuple-element.17.conv_ref, f32[3,512]{1,0:T(4,128)} %cw_ref.3, f32[1,512]{1,0:T(1,128)} %bitcast.2, ...), custom_call_target="tpu_custom_call" | custom-call | tf_op jit(solution)/shard_map/backward_attention/pallas_call | solution.py:731
  161.7 1.7 %copy.16 = bf16[1024,64]{0,1:T(8,128)(2,1)} copy(bf16[1024,64]{1,0:T(8,128)(2,1)} %get-tuple-element.26) | data formatting | bytes 262144
  163.4 1.7 %copy.17 = bf16[1024,64]{0,1:T(8,128)(2,1)} copy(bf16[1024,64]{1,0:T(8,128)(2,1)} %get-tuple-element.27) | data formatting | bytes 262144
  165.2 0.0 copy-done
  165.2 0.0 copy-start.1
  165.2 1.3 copy.21
  166.5 0.6 copy-done.1
  167.1 0.0 copy-start.2
  167.1 1.0 copy.22
  168.1 0.1 copy-done.2
  168.2 0.7 copy.23
Async XLA Ops:
  128.2 37.0 %copy-start = (bf16[1024,1024]{1,0:T(8,128)(2,1)S(1)}, bf16[1024,1024]{1,0:T(8,128)(2,1)}, u32[]{:S(2)}) copy-start(bf16[1024,1024]{1,0:T(8,128)(2,1)} %get-tuple-element.35) | copy-start | bytes 6291460
  165.2 2.0 %copy-start.1 = (bf16[1024,512]{1,0:T(8,128)(2,1)S(1)}, bf16[1024,512]{1,0:T(8,128)(2,1)}, u32[]{:S(2)}) copy-start(bf16[1024,512]{1,0:T(8,128)(2,1)} %get-tuple-element.38) | copy-start | bytes 3145732
  167.1 1.0 copy-start.2

commit v2 on v0

v2 whole, which is shorter than its diff:
```python
import functools

import jax
import jax.numpy as jnp
from jax import lax
from jax.experimental import pallas as pl
from jax.experimental.pallas import tpu as pltpu
from jax.sharding import PartitionSpec as P

f32 = jnp.float32
bf16 = jnp.bfloat16
FD = 16
BLOCK = 256
ROWS = 1024
HEADS = 4
NB = ROWS // BLOCK
DV = 128
CH = HEADS * DV
FEAT = 1024
NF = 160
EPSILON = 1e-05
VMEM_LIMIT = 60 * 1024 * 1024


def nn(a, b):
    return lax.dot_general(a, b, (((1,), (0,)), ((), ())), preferred_element_type=f32)


def nt(a, b):
    return lax.dot_general(a, b, (((1,), (1,)), ((), ())), preferred_element_type=f32)


def tn(a, b):
    return lax.dot_general(a, b, (((0,), (0,)), ((), ())), preferred_element_type=f32)


def place():
    s = lax.axis_index("seq")
    z = lax.axis_index("head")
    return s, z, s // 8, (s // 2) % 4, s % 2


def seq_of(x, y, c):
    return (x * 4 + y) * 2 + c


def remote(src, dst, send_sem, recv_sem, seq, head):
    copy = pltpu.make_async_remote_copy(
        src_ref=src,
        dst_ref=dst,
        send_sem=send_sem,
        recv_sem=recv_sem,
        device_id={"seq": seq, "head": head},
        device_id_type=pl.DeviceIdType.MESH,
    )
    copy.start()
    return copy


def greet(devices):
    barrier = pltpu.get_barrier_semaphore()
    for seq, head in devices:
        pl.semaphore_signal(
            barrier, inc=1, device_id={"seq": seq, "head": head}, device_id_type=pl.DeviceIdType.MESH
        )
    pl.semaphore_wait(barrier, len(devices))


def plane_peers(s, z, x, y, c):
    out = [(seq_of(x, y, 1 - c), z)]
    for j in (1, 2, 3):
        out.append((seq_of((x + j) % 4, y, c), z))
        out.append((seq_of(x, (y + j) % 4, c), z))
    return out


def spread(xt_ref, x2_ref):
    for h in range(HEADS):
        x = xt_ref[16 * h : 16 * h + 16, :].astype(f32)
        x2_ref[h, 0:16, :] = x
        x2_ref[h, 16:32, :] = x


def phi(x2_ref, h, cols):
    x = x2_ref[h, 0:16, cols]
    parts = [x * x]
    for d in range(1, 8):
        parts.append(x * x2_ref[h, d : d + 16, cols])
    parts.append(x[0:8] * x2_ref[h, 8:16, cols])
    parts.append((lax.broadcasted_iota(jnp.int32, (8, BLOCK), 0) == 0).astype(f32))
    parts.append(x)
    return jnp.concatenate(parts, axis=0).astype(bf16)


def phi_back(g, x2_ref, t2_ref, h, cols):
    x = x2_ref[h, 0:16, cols]
    acc = g[144:160] + 2.0 * g[0:16] * x
    for d in range(1, 8):
        gd = g[16 * d : 16 * d + 16]
        acc = acc + gd * x2_ref[h, d : d + 16, cols]
        t = gd * x
        t2_ref[d - 1, 0:16, :] = t
        t2_ref[d - 1, 16:32, :] = t
        acc = acc + t2_ref[d - 1, 16 - d : 32 - d, :]
    g8 = g[128:136]
    low = g8 * x2_ref[h, 8:16, cols]
    high = g8 * x[0:8]
    return acc + jnp.concatenate([low, high], axis=0)


def weights():
    r = lax.broadcasted_iota(jnp.int32, (NF, DV), 0)
    return jnp.where(
        r < 16, 1.0 / 32, jnp.where(r < 136, 1.0 / 16, jnp.where(r < 144, 1.0, 0.25))
    ).astype(f32)


def lower():
    r = lax.broadcasted_iota(jnp.int32, (BLOCK, BLOCK), 0)
    c = lax.broadcasted_iota(jnp.int32, (BLOCK, BLOCK), 1)
    return r >= c


SCAN_SCRATCH = [
    pltpu.VMEM((HEADS, NF, DV), f32),
    pltpu.VMEM((2, NF, DV), f32),
    pltpu.VMEM((2, NF, DV), bf16),
    pltpu.VMEM((3, 2, NF, DV), bf16),
    pltpu.VMEM((2, NF, DV), bf16),
    pltpu.VMEM((3, 2, NF, DV), bf16),
    pltpu.VMEM((2, NF, DV), f32),
    pltpu.VMEM((2, NF, DV), f32),
    pltpu.VMEM((2, NF, DV), f32),
    pltpu.VMEM((HEADS, NF, DV), f32),
    pltpu.SemaphoreType.DMA((8,)),
    pltpu.SemaphoreType.DMA((8,)),
]


def scan_steps(refs, forward):
    tot, ra, ys, yr, xs, xr, py, fs, fr, ent, ssem, rsem = refs
    s, z, x, y, c = place()
    sibling = seq_of(x, y, 1 - c)
    mine = pl.ds(2 * c, 2)
    copies = {}

    def counts(me, j):
        met = (me - j >= 0) if forward else (me - j < 0)
        return jnp.where(met, 1.0, 0.0).astype(f32)

    def pair():
        copies["a"] = remote(tot.at[pl.ds(2 * (1 - c), 2)], ra, ssem.at[0], rsem.at[0], sibling, z)

    def along_y():
        copies["a"].wait_recv()
        ys[...] = (tot[mine] + ra[...]).astype(bf16)
        for j in (1, 2, 3):
            copies["y", j] = remote(
                ys, yr.at[j - 1], ssem.at[j], rsem.at[j], seq_of(x, (y + j) % 4, c), z
            )

    def along_x():
        row = tot[mine] + ra[...]
        before = jnp.zeros((2, NF, DV), f32)
        for j in (1, 3, 2):
            copies["y", j].wait_recv()
            got = yr[j - 1].astype(f32)
            row = row + got
            before = before + got * counts(y, j)
        xs[...] = row.astype(bf16)
        py[...] = before
        for j in (1, 2, 3):
            copies["x", j] = remote(
                xs, xr.at[j - 1], ssem.at[3 + j], rsem.at[3 + j], seq_of((x + j) % 4, y, c), z
            )

    def back():
        before = py[...]
        for j in (1, 3, 2):
            copies["x", j].wait_recv()
            before = before + xr[j - 1].astype(f32) * counts(x, j)
        first = jnp.where(c == 0, 1.0, 0.0).astype(f32)
        other = first if forward else 1.0 - first
        fs[...] = before + tot[mine] * other
        ent[mine] = before + ra[...] * (1.0 - other)
        copies["f"] = remote(fs, fr, ssem.at[7], rsem.at[7], sibling, z)

    def done():
        copies["f"].wait_recv()
        ent[pl.ds(2 * (1 - c), 2)] = fr[...]
        for copy in copies.values():
            copy.wait_send()

    return pair, along_y, along_x, back, done


SLOT = {2: 0, 1: 1, 3: 2, 0: 3}
GROUPS = ((2,), (1, 3))


def row_block(n):
    return pl.ds(pl.multiple_of(n * BLOCK, BLOCK), BLOCK)


def kernel(
    qt_ref, kt_ref, v_ref, cw_ref, gain_ref, w_hbm, cot_hbm,
    mixed_ref, gq_ref, gk_ref, gv_ref, gw_ref,
    halo, halo_back, edge_rows, wide, qx, kx, conv, st, hid, prev, oall,
    wt, cot, cott, opp, to_r, to_l, opp_l, opp_r, from_r, from_l,
    gwp, r1, gsum, p1a, p1b, s2a, s2b, p2a, p2b, fin, macc,
    gh, bg, fw, dx, t2,
    lsem, hsem, zs, zr, ws, wr, gs, gr, ms, mr, *scans,
):
    s, z, x, y, c = place()
    right, left = (z + 1) % 4, (z + 3) % 4
    sibling = seq_of(x, y, 1 - c)
    after, before = (s + 1) % 32, (s + 31) % 32
    sends = []

    def go(*args):
        copy = remote(*args)
        sends.append(copy)
        return copy

    barrier = pltpu.get_barrier_semaphore()

    def signal(seq, head):
        pl.semaphore_signal(
            barrier, inc=1, device_id={"seq": seq, "head": head}, device_id_type=pl.DeviceIdType.MESH
        )

    known = plane_peers(s, z, x, y, c) + [(s, (z + k) % 4) for k in (1, 2, 3)]
    known += [(after, z), (before, z)]
    known += [(seq_of(z, y, c), (z + k) % 4) for k in (1, 2, 3)]
    known += [(seq_of((x + j) % 4, y, c), x) for j in (1, 2, 3)]
    for seq, head in known:
        signal(seq, head)
    stays = x == z

    @pl.when(jnp.logical_not(stays))
    def _():
        signal(seq_of(z, y, c), z)
        signal(s, x)

    pl.semaphore_wait(barrier, len(known) + jnp.where(stays, 0, 2))

    row = c * 512 + x * 128 + y * 32
    wz = {}
    for k in (2, 1, 3):
        there = (z + k) % 4
        wz[k] = go(
            w_hbm.at[pl.ds(pl.multiple_of(there * FEAT + row, 32), 32)],
            wt.at[SLOT[4 - k], pl.ds(pl.multiple_of(row, 32), 32)],
            ws.at[k - 1],
            wr.at[k - 1],
            s,
            there,
        )
    edge = go(v_ref.at[pl.ds(ROWS - 16, 16)], halo, hsem.at[0], hsem.at[1], after, z)
    load_cot = pltpu.make_async_copy(cot_hbm, cot, lsem.at[0])
    load_cot.start()
    load_w = pltpu.make_async_copy(
        w_hbm.at[pl.ds(pl.multiple_of(z * FEAT, FEAT), FEAT)], wt.at[SLOT[0]], lsem.at[1]
    )
    load_w.start()

    def piece(group, px, py, half):
        at = pl.multiple_of(c * 512 + px * 128 + py * 32, 32)
        slots = pl.ds(0, 1) if group == 0 else pl.ds(1, 2)
        return wt.at[slots, pl.ds(at, 32), pl.ds(half * 256, 256)]

    w1, w2, w3 = {}, {}, {}

    def w_first(group):
        for k in GROUPS[group]:
            wz[4 - k].wait_recv()
        at = 3 + 31 * group
        for j in (1, 2, 3):
            own = piece(group, x, y, 0)
            i = at + j - 1
            w1[group, 0, j] = go(own, own, ws.at[i], wr.at[i], seq_of((x + j) % 4, y, c), z)
            own = piece(group, x, y, 1)
            i = at + j + 2
            w1[group, 1, j] = go(own, own, ws.at[i], wr.at[i], seq_of(x, (y + j) % 4, c), z)

    def w_second(group):
        at = 9 + 31 * group
        for i in (0, 1, 3, 2):
            for half in (0, 1):
                if i:
                    w1[group, half, i].wait_recv()
                if half == 0:
                    block = piece(group, (x - i + 4) % 4, y, 0)
                else:
                    block = piece(group, x, (y - i + 4) % 4, 1)
                for j in (1, 2, 3):
                    to = seq_of(x, (y + j) % 4, c) if half == 0 else seq_of((x + j) % 4, y, c)
                    w2[group, half, i, j] = go(block, block, ws.at[at], wr.at[at], to, z)
                    at += 1

    def w_third(group):
        for (which, *_), copy in w2.items():
            if which == group:
                copy.wait_recv()
        slots = pl.ds(0, 1) if group == 0 else pl.ds(1, 2)
        half = wt.at[slots, pl.ds(pl.multiple_of(c * 512, 512), 512)]
        i = 33 + 31 * group
        w3[group] = go(half, half, ws.at[i], wr.at[i], sibling, z)

    spread(kt_ref, kx)
    spread(qt_ref, qx)
    w_first(0)
    wide[8 : 8 + ROWS, :] = v_ref[...].astype(f32)
    w_first(1)
    edge.wait_recv()
    inside = jnp.where(s > 0, 1.0, 0.0).astype(f32)
    wide[0:8, :] = halo[...].astype(f32)[8:16] * inside

    def convolve(n):
        at = 8 + n * BLOCK
        acc = cw_ref[0:1, :] * wide[at : at + BLOCK, :]
        for j in (1, 2):
            acc = acc + cw_ref[j : j + 1, :] * wide[at - j : at - j + BLOCK, :]
        conv[n * BLOCK : (n + 1) * BLOCK, :] = acc.astype(bf16)

    convolve(0)
    w_second(0)
    for n in (1, 2, 3):
        convolve(n)
    w_second(1)
    load_cot.wait()

    def flip(b, carry):
        cott[:, row_block(b)] = jnp.transpose(cot[row_block(b), :], (1, 0))
        return carry

    lax.fori_loop(0, NB, flip, 0)
    w_third(0)

    scan_a, scan_b = scans[: len(scans) // 2], scans[len(scans) // 2 :]
    tot, ent = scan_a[0], scan_a[9]
    tot[...] = jnp.zeros_like(tot)

    def states(n, carry):
        rows = row_block(n)
        for h in range(HEADS):
            own = nn(phi(kx, h, rows), conv[rows, h * DV : (h + 1) * DV])
            st[n, h] = own
            tot[h] += own
        return carry

    lax.fori_loop(0, NB, states, 0)
    pair, along_y, along_x, back, done = scan_steps(scan_a, True)
    pair()

    def fill(k, dst, lo, hi):
        def part(b, carry):
            rows = row_block(b)
            dst[rows, :] = nn(cot[rows, :], wt[SLOT[k]]).astype(bf16)
            return carry

        lax.fori_loop(lo, hi, part, 0)

    half_a, half_b = pl.ds(0, 512), pl.ds(512, 512)
    rs = {}
    w3[0].wait_recv()
    fill(2, opp, 0, 4)
    rs["or"] = go(opp.at[half_a], opp_l, zs.at[12], zr.at[12], s, right)
    rs["ol"] = go(opp.at[half_b], opp_r, zs.at[13], zr.at[13], s, left)
    w_third(1)
    along_y()
    mask = lower()
    mask_t = jnp.logical_not(mask) | (
        lax.broadcasted_iota(jnp.int32, (BLOCK, BLOCK), 0)
        == lax.broadcasted_iota(jnp.int32, (BLOCK, BLOCK), 1)
    )

    def intra(n, carry):
        rows = row_block(n)
        for h in range(HEADS):
            entries = slice(16 * h, 16 * h + 16)
            sc = tn(qt_ref[entries, rows], kt_ref[entries, rows])
            att = jnp.where(mask, 1.0 + sc * (0.25 + sc * (1.0 / 32)), 0.0).astype(bf16)
            hid[rows, h * DV : (h + 1) * DV] = nn(att, conv[rows, h * DV : (h + 1) * DV])
        return carry

    lax.fori_loop(0, 2, intra, 0)
    w3[1].wait_recv()
    fill(1, to_r, 2, 4)
    rs["dr"] = go(to_r.at[half_b], from_l.at[half_b], zs.at[14], zr.at[14], s, right)
    fill(3, to_l, 0, 2)
    rs["dl"] = go(to_l.at[half_a], from_r.at[half_a], zs.at[15], zr.at[15], s, left)
    along_x()
    lax.fori_loop(2, 4, intra, 0)
    back()
    done()
    wts = weights()

    def finish(n, carry):
        rows = row_block(n)
        for h in range(HEADS):
            lanes = slice(h * DV, (h + 1) * DV)
            state = ent[h]
            ent[h] = state + st[n, h]
            before_block = (state * wts).astype(bf16)
            prev[n, h] = before_block
            hidden = hid[rows, lanes] + tn(phi(qx, h, rows), before_block)
            hid[rows, lanes] = hidden
            scale = lax.rsqrt(jnp.mean(hidden * hidden, axis=-1, keepdims=True) + EPSILON)
            oall[0, h, rows, :] = (hidden * scale * gain_ref[0:1, lanes]).astype(bf16)
        return carry

    lax.fori_loop(0, NB, finish, 0)

    def add_in(k, dst, got, lo):
        def part(b, carry):
            rows = row_block(lo + b)
            here = row_block(b)
            term = nn(cot[rows, :], wt[SLOT[k]]) + got[here, :].astype(f32)
            dst[rows, :] = term.astype(bf16)
            return carry

        lax.fori_loop(0, 2, part, 0)

    rs["or"].wait_recv()
    add_in(1, to_r, opp_l, 0)
    rs["ar"] = go(to_r.at[half_a], from_l.at[half_a], zs.at[16], zr.at[16], s, right)
    rs["ol"].wait_recv()
    add_in(3, to_l, opp_r, 2)
    rs["al"] = go(to_l.at[half_b], from_r.at[half_b], zs.at[17], zr.at[17], s, left)

    ag = {}
    for h in range(HEADS):
        ag["l", h] = go(oall.at[0, h], oall.at[3, h], zs.at[h], zr.at[h], s, right)
        e = (h + 2) % 4
        ag["r", e] = go(oall.at[0, e], oall.at[1, e], zs.at[4 + e], zr.at[4 + e], s, left)

    def hand_on(h):
        ag["l", h].wait_recv()
        ag["f", h] = go(oall.at[3, h], oall.at[2, h], zs.at[8 + h], zr.at[8 + h], s, right)
        e = h + 2
        ag["r", e].wait_recv()
        ag["f", e] = go(oall.at[1, e], oall.at[2, e], zs.at[8 + e], zr.at[8 + e], s, left)

    def four(k, rows):
        return jnp.concatenate([oall[k, h, rows, :] for h in range(HEADS)], axis=1)

    g1, g2, g3, g4 = {}, {}, {}, {}

    def gw_term(k):
        def part(t, carry):
            term = nn(cott[row_block(t), :], four(k, slice(None))).astype(bf16)
            gwp[0, k, t] = term[0:128]
            gwp[1, k, t] = term[128:256]
            return carry

        lax.fori_loop(0, 4, part, 0)
        g1[k] = go(gwp.at[1 - c, k], r1.at[k], gs.at[k], gr.at[k], sibling, z)

    def gw_first(k):
        g1[k].wait_recv()

        def part(t, carry):
            gsum[k, t] = (gwp[c, k, t].astype(f32) + r1[k, t].astype(f32)).astype(bf16)
            return carry

        lax.fori_loop(0, 4, part, 0)
        for j in (1, 2, 3):
            nx, ny = (x + j) % 4, (y + j) % 4
            i = 4 + 12 * k + j - 1
            rows = pl.ds(pl.multiple_of(nx * 32, 32), 32)
            g2[k, 0, j] = go(
                gsum.at[k, :, rows, pl.ds(0, 256)],
                p1a.at[k, j - 1], gs.at[i], gr.at[i], seq_of(nx, y, c), z,
            )
            i += 3
            g2[k, 1, j] = go(
                gsum.at[k, ny, :, pl.ds(256, 256)],
                p1b.at[k, j - 1], gs.at[i], gr.at[i], seq_of(x, ny, c), z,
            )

    my_rows = pl.ds(pl.multiple_of(x * 32, 32), 32)

    def gw_second(k):
        sum_a = gsum[k, :, my_rows, 0:256].astype(f32)
        sum_b = gsum[k, y, :, 256:512].astype(f32)
        for j in (1, 3, 2):
            g2[k, 0, j].wait_recv()
            sum_a = sum_a + p1a[k, j - 1].astype(f32)
            g2[k, 1, j].wait_recv()
            sum_b = sum_b + p1b[k, j - 1].astype(f32)
        s2a[k] = sum_a.astype(bf16)
        s2b[k] = sum_b.astype(bf16)
        for j in (1, 2, 3):
            nx, ny = (x + j) % 4, (y + j) % 4
            i = 4 + 12 * k + 6 + j - 1
            rows = pl.ds(pl.multiple_of(nx * 32, 32), 32)
            g3[k, 0, j] = go(
                s2a.at[k, ny], p2a.at[k, j - 1], gs.at[i], gr.at[i], seq_of(x, ny, c), z
            )
            i += 3
            g3[k, 1, j] = go(
                s2b.at[k, rows], p2b.at[k, j - 1], gs.at[i], gr.at[i], seq_of(nx, y, c), z
            )

    def gw_third(k):
        sum_a = s2a[k, y].astype(f32)
        sum_b = s2b[k, my_rows, :].astype(f32)
        for j in (1, 3, 2):
            g3[k, 0, j].wait_recv()
            sum_a = sum_a + p2a[k, j - 1].astype(f32)
            g3[k, 1, j].wait_recv()
            sum_b = sum_b + p2b[k, j - 1].astype(f32)
        fin[k, :, 0:256] = sum_a.astype(bf16)
        fin[k, :, 256:512] = sum_b.astype(bf16)

        def move():
            return pltpu.make_async_remote_copy(
                src_ref=fin.at[k],
                dst_ref=gw_ref.at[my_rows],
                send_sem=ms.at[k],
                recv_sem=mr.at[x],
                device_id={"seq": seq_of(z, y, c), "head": (z + k) % 4},
                device_id_type=pl.DeviceIdType.MESH,
            )

        if k:
            g4[k] = move
            move().start()
        else:

            @pl.when(stays)
            def _():
                gw_ref[my_rows, :] = fin[0]

            @pl.when(jnp.logical_not(stays))
            def _():
                move().start()
                move().wait_send()

    def gw_done():
        for k in (1, 2, 3):
            g4[k]().wait_send()
        for xs in range(4):

            @pl.when(jnp.logical_not(stays & (x == xs)))
            def _():
                pltpu.make_async_remote_copy(
                    src_ref=fin.at[0],
                    dst_ref=gw_ref.at[pl.ds(32 * xs, 32)],
                    send_sem=ms.at[0],
                    recv_sem=mr.at[xs],
                    device_id={"seq": seq_of(z, y, c), "head": (z + 1) % 4},
                    device_id_type=pl.DeviceIdType.MESH,
                ).wait_recv()

    def mix(ks, first, last):
        def part(b, carry):
            rows = row_block(b)
            for u in (0, 1):
                cols = slice(512 * u, 512 * u + 512)
                acc = None if first else macc[rows, cols]
                for k in ks:
                    term = nt(four(k, rows), wt[SLOT[k], cols, :])
                    acc = term if acc is None else acc + term
                if last:
                    mixed_ref[rows, cols] = acc.astype(bf16)
                else:
                    macc[rows, cols] = acc
            return carry

        lax.fori_loop(0, NB, part, 0)

    gw_term(0)
    load_w.wait()
    mix((0,), True, False)
    gw_first(0)

    for name in ("dr", "dl", "ar", "al"):
        rs[name].wait_recv()
    tot_b, ent_b = scan_b[0], scan_b[9]
    tot_b[...] = jnp.zeros_like(tot_b)

    def back_states(n, carry):
        rows = row_block(n)
        grad_out = nn(cot[rows, :], wt[SLOT[0]])
        grad_out = grad_out + from_r[rows, :].astype(f32) + from_l[rows, :].astype(f32)
        for h in range(HEADS):
            lanes = slice(h * DV, (h + 1) * DV)
            hidden = hid[rows, lanes]
            scale = lax.rsqrt(jnp.mean(hidden * hidden, axis=-1, keepdims=True) + EPSILON)
            normed = hidden * scale
            up = grad_out[:, lanes] * gain_ref[0:1, lanes]
            grad = scale * (up - normed * jnp.mean(up * normed, axis=-1, keepdims=True))
            grad = grad.astype(bf16)
            gh[rows, lanes] = grad
            own = nn(phi(qx, h, rows), grad)
            bg[n, h] = own
            tot_b[h] += own
        return carry

    lax.fori_loop(0, NB, back_states, 0)
    pair, along_y, along_x, back, done = scan_steps(scan_b, False)

    def back_intra(n, carry):
        rows = row_block(n)
        for h in range(HEADS):
            lanes = slice(h * DV, (h + 1) * DV)
            entries = slice(16 * h, 16 * h + 16)
            qh = qt_ref[entries, rows]
            kh = kt_ref[entries, rows]
            g = gh[rows, lanes]
            v = conv[rows, lanes]
            sc = tn(kh, qh)
            ds = jnp.where(mask_t, nt(v, g) * (0.25 + sc * (1.0 / 16)), 0.0).astype(bf16)
            att = jnp.where(mask_t, 1.0 + sc * (0.25 + sc * (1.0 / 32)), 0.0).astype(bf16)
            wide[rows, lanes] = nn(att, g)
            across = phi_back(nt(prev[n, h], g), qx, t2, h, rows)
            gq_ref[entries, rows] = (nn(kh, ds) + across).astype(bf16)
            dx[entries, rows] = nt(qh, ds)
        return carry

    pair()
    lax.fori_loop(0, 1, back_intra, 0)
    along_y()
    hand_on(0)
    lax.fori_loop(1, 3, back_intra, 0)
    along_x()
    hand_on(1)
    lax.fori_loop(3, 4, back_intra, 0)
    back()
    gw_second(0)
    done()

    def suffix(t, carry):
        n = NB - 1 - t
        for h in range(HEADS):
            state = ent_b[h]
            ent_b[h] = state + bg[n, h]
            fw[n, h] = (state * wts).astype(bf16)
        return carry

    lax.fori_loop(0, NB, suffix, 0)

    def back_finish(n, carry):
        rows = row_block(n)
        for h in range(HEADS):
            lanes = slice(h * DV, (h + 1) * DV)
            entries = slice(16 * h, 16 * h + 16)
            wide[rows, lanes] += tn(phi(kx, h, rows), fw[n, h])
            across = phi_back(nt(fw[n, h], conv[rows, lanes]), kx, t2, h, rows)
            gk_ref[entries, rows] = (dx[entries, rows] + across).astype(bf16)
        return carry

    lax.fori_loop(0, 1, back_finish, 0)
    edge_rows[...] = wide[0:8, :]
    edge_back = go(edge_rows, halo_back, hsem.at[2], hsem.at[3], before, z)
    lax.fori_loop(1, NB, back_finish, 0)
    edge_back.wait_recv()
    inside = jnp.where(s < 31, 1.0, 0.0).astype(f32)
    wide[ROWS : ROWS + 8, :] = halo_back[...] * inside
    for n in range(NB):
        at = n * BLOCK
        acc = cw_ref[0:1, :] * wide[at : at + BLOCK, :]
        for j in (1, 2):
            acc = acc + cw_ref[j : j + 1, :] * wide[at + j : at + j + BLOCK, :]
        gv_ref[at : at + BLOCK, :] = acc.astype(bf16)

    gw_third(0)
    ag["l", 2].wait_recv()
    ag["l", 3].wait_recv()
    gw_term(3)
    ag["r", 0].wait_recv()
    ag["r", 1].wait_recv()
    gw_term(1)
    gw_first(3)
    gw_first(1)
    mix((1, 3), False, False)
    gw_second(3)
    gw_second(1)
    for h in range(HEADS):
        ag["f", h].wait_recv()
    gw_term(2)
    gw_third(3)
    gw_third(1)
    gw_first(2)
    mix((2,), False, True)
    gw_second(2)
    gw_third(2)
    gw_done()
    for copy in sends:
        copy.wait_send()


def on_device(query, key_feat, values, conv_w, gain, w_out, cotangent):
    vm = pl.BlockSpec(memory_space=pltpu.VMEM)
    hbm = pl.BlockSpec(memory_space=pl.ANY)
    dma = pltpu.SemaphoreType.DMA
    vmem = pltpu.VMEM
    mixed, gq, gk, gv, gw = pl.pallas_call(
        kernel,
        out_shape=(
            jax.ShapeDtypeStruct((ROWS, FEAT), bf16),
            jax.ShapeDtypeStruct((HEADS * FD, ROWS), bf16),
            jax.ShapeDtypeStruct((HEADS * FD, ROWS), bf16),
            jax.ShapeDtypeStruct((ROWS, CH), bf16),
            jax.ShapeDtypeStruct((128, CH), bf16),
        ),
        in_specs=[vm] * 5 + [hbm] * 2,
        out_specs=(vm,) * 5,
        scratch_shapes=[
            vmem((16, CH), bf16),
            vmem((8, CH), f32),
            vmem((8, CH), f32),
            vmem((ROWS + 8, CH), f32),
            vmem((HEADS, 32, ROWS), f32),
            vmem((HEADS, 32, ROWS), f32),
            vmem((ROWS, CH), bf16),
            vmem((NB, HEADS, NF, DV), f32),
            vmem((ROWS, CH), f32),
            vmem((NB, HEADS, NF, DV), bf16),
            vmem((4, HEADS, ROWS, DV), bf16),
            vmem((4, FEAT, CH), bf16),
            vmem((ROWS, FEAT), bf16),
            vmem((FEAT, ROWS), bf16),
            vmem((ROWS, CH), bf16),
            vmem((ROWS, CH), bf16),
            vmem((ROWS, CH), bf16),
            vmem((512, CH), bf16),
            vmem((512, CH), bf16),
            vmem((ROWS, CH), bf16),
            vmem((ROWS, CH), bf16),
            vmem((2, 4, 4, 128, CH), bf16),
            vmem((4, 4, 128, CH), bf16),
            vmem((4, 4, 128, CH), bf16),
            vmem((4, 3, 4, 32, 256), bf16),
            vmem((4, 3, 128, 256), bf16),
            vmem((4, 4, 32, 256), bf16),
            vmem((4, 128, 256), bf16),
            vmem((4, 3, 32, 256), bf16),
            vmem((4, 3, 32, 256), bf16),
            vmem((4, 32, CH), bf16),
            vmem((ROWS, FEAT), f32),
            vmem((ROWS, CH), bf16),
            vmem((NB, HEADS, NF, DV), f32),
            vmem((NB, HEADS, NF, DV), bf16),
            vmem((HEADS * FD, ROWS), f32),
            vmem((7, 32, BLOCK), f32),
            dma((2,)),
            dma((4,)),
            dma((18,)),
            dma((18,)),
            dma((65,)),
            dma((65,)),
            dma((52,)),
            dma((52,)),
            dma((4,)),
            dma((4,)),
        ]
        + SCAN_SCRATCH * 2,
        compiler_params=pltpu.CompilerParams(
            collective_id=0, has_side_effects=True, vmem_limit_bytes=VMEM_LIMIT
        ),
        name="sublayer",
    )(query.T, key_feat.T, values, conv_w, gain.reshape(1, CH), w_out, cotangent)
    return mixed, gq.T, gk.T, gv, gw


def solution(mesh):
    both = P("seq", "head")
    return jax.shard_map(
        on_device,
        mesh=mesh,
        in_specs=(both, both, both, P(None, "head"), P("head"), P(None, "head"), both),
        out_specs=(both,) * 5,
        check_vma=False,
    )
```

time: 454 us -> 127 us (0.28)
  waiting for transfers between devices: 294 us -> 0 us
  Pallas kernels: 0 us -> 119 us
  matrix products: 55 us -> 0 us
  other arithmetic: 53.1 us -> 0 us
  local copies, waits for them, and re-layouts: 26.5 us -> 6.13 us
  between operations: 14.4 us -> 0.67 us
  starting transfers between devices: 6.61 us -> 0 us
    all_gather x3 -> x0, waiting for transfers between devices: 158 us -> none  [the longest x1 67.9 us: entering(): gathered = lax.all_gather(part, axis)]
    pallas_call x0 -> x1, Pallas kernels: none -> 119 us  [on_device(): pl.pallas_call(kernel, out_shape=(jax.ShapeDtypeStruct((ROWS, FEAT), bf16...]
    reduce_scatter x1 -> x0, waiting for transfers between devices: 83.5 us -> none  [on_device(): lax.psum_scatter(partial_out.astype(jnp.bfloat16), 'head', scatter_dimens...]
    dot_general x15 -> x0, matrix products: 55 us -> none  [the longest x1 9.62 us: on_device(): lax.dot_general(cot_full, out_heads, (((0,), (0,)), ((), ())), preferred_...]
    unnamed x6 -> x0, waiting for transfers between devices: 51.3 us -> none
    add x31 -> x0, other arithmetic: 34.9 us -> none  [add_states(): return earlier + later]
    convert_element_type x7 -> x0, other arithmetic: 6.83 us -> none  [the longest x1 1.86 us: on_device(): out_heads = from_blocks((normed * gain_blocks).astype(bf16))]
    ppermute x2 -> x0, starting transfers between devices: 6.23 us -> none  [from_behind(): return lax.ppermute(block, axis, route)]
  transfers between devices with their start and end apart: 7 -> 0, of which waited for: 6 -> 0; matrix products, arithmetic and copies ran while one was open for 23% -> 0% of each run, Pallas kernels for 0% -> 0%
where the time goes in v2:
time: 127 us; the launch traced here: 126 us
  Pallas kernels  119 us (94%)
  local copies, waits for them, and re-layouts  6.13 us (5%)
    pallas_call x1, Pallas kernels, on_device(): pl.pallas_call(kernel, out_shape=(jax.ShapeDtypeStruct((ROWS, FEAT), bf16...  119 us
    unnamed x13, local copies, waits for them, and re-layouts  6.13 us

profile of v2, /device:TPU:4, one launch (start us, length us, event | category | flops | bytes accessed | tf_op | source)
XLA Modules:
  0.0 126.2 jit_solution(17045632694307487965)
XLA Ops:
  0.6 119.4 %sublayer.1 = (bf16[1024,1024]{1,0:T(8,128)(2,1)}, bf16[64,1024]{1,0:T(8,128)(2,1)}, bf16[64,1024]{1,0:T(8,128)(2,1)}, bf16[1024,512]{1,0:T(8,128)(2,1)}, bf16[128,512]{1,0:T(8,128)(2,1)}) custom-call(bf16[64,1024]{1,0:T(8,128)(2,1)} %bitcast.5, bf16[64,1024]{1,0:T(8,128)(2,1)} %bitcast.6, bf16[1024,512]{1,0:T(8,128)(2,1)} %v_ref.1, f32[3,512]{1,0:T(4,128)} %cw_ref.1, ...), custom_call_target="tpu_custom_call" | custom-call | tf_op jit(solution)/shard_map/sublayer/pallas_call | solution.py:700
  120.0 0.0 copy-start.3
  120.0 0.0 copy-start.2
  120.0 0.0 copy-start
  120.0 3.2 %copy.17 = bf16[1024,1024]{1,0:T(8,128)(2,1)} copy(bf16[1024,1024]{1,0:T(8,128)(2,1)} %get-tuple-element.20) | data formatting | bytes 4194304
  123.2 0.0 copy-done.3
  123.2 0.0 copy-start.1
  123.2 0.7 copy.18
  123.9 0.0 copy-done.2
  123.9 0.7 copy.19
  124.5 0.0 copy-done
  124.5 1.0 copy.20
  125.5 0.0 copy-done.1
  125.5 0.7 copy.21
Async XLA Ops:
  120.0 3.2 %copy-start.3 = (bf16[64,1024]{1,0:T(8,128)(2,1)S(1)}, bf16[64,1024]{1,0:T(8,128)(2,1)}, u32[]{:S(2)}) copy-start(bf16[64,1024]{1,0:T(8,128)(2,1)} %get-tuple-element.11) | copy-start | bytes 393220
  120.0 3.9 %copy-start.2 = (bf16[64,1024]{1,0:T(8,128)(2,1)S(1)}, bf16[64,1024]{1,0:T(8,128)(2,1)}, u32[]{:S(2)}) copy-start(bf16[64,1024]{1,0:T(8,128)(2,1)} %get-tuple-element.12) | copy-start | bytes 393220
  120.0 4.5 %copy-start = (bf16[1024,512]{1,0:T(8,128)(2,1)S(1)}, bf16[1024,512]{1,0:T(8,128)(2,1)}, u32[]{:S(2)}) copy-start(bf16[1024,512]{1,0:T(8,128)(2,1)} %get-tuple-element.23) | copy-start | bytes 3145732
  123.2 2.3 %copy-start.1 = (bf16[128,512]{1,0:T(8,128)(2,1)S(1)}, bf16[128,512]{1,0:T(8,128)(2,1)}, u32[]{:S(2)}) copy-start(bf16[128,512]{1,0:T(8,128)(2,1)} %get-tuple-element.24) | copy-start | bytes 393220

commit v3 on v2

--- a/solution.py
+++ b/solution.py
@@ -196,6 +196,16 @@
 
 SLOT = {2: 0, 1: 1, 3: 2, 0: 3}
 GROUPS = ((2,), (1, 3))
+FILL = 256
+REST = ROWS - FILL
+HALF = REST // 2
+UNITS = {
+    "0": (0, (0, 1, 2, 3), 0, 256),
+    "1": (1, (0, 1, 2, 3), 0, 256),
+    "3": (3, (0, 1, 2, 3), 0, 256),
+    "2a": (2, (0, 2), 0, 128),
+    "2b": (2, (1, 3), 128, 128),
+}
 
 
 def row_block(n):
@@ -203,13 +213,13 @@
 
 
 def kernel(
-    qt_ref, kt_ref, v_ref, cw_ref, gain_ref, w_hbm, cot_hbm,
-    mixed_ref, gq_ref, gk_ref, gv_ref, gw_ref,
+    qt_ref, kt_ref, cw_ref, gain_ref, v_hbm, w_hbm, cot_hbm,
+    mixed_hbm, gq_hbm, gk_hbm, gv_hbm, gw_ref,
     halo, halo_back, edge_rows, wide, qx, kx, conv, st, hid, prev, oall,
-    wt, cot, cott, opp, to_r, to_l, opp_l, opp_r, from_r, from_l,
-    gwp, r1, gsum, p1a, p1b, s2a, s2b, p2a, p2b, fin, macc,
-    gh, bg, fw, dx, t2,
-    lsem, hsem, zs, zr, ws, wr, gs, gr, ms, mr, *scans,
+    wt, cot, cott, opp, to_r, to_l, opp_l, opp_r, from_r, from_l, cf, gf,
+    pool, r1, gsum, p1a, p1b, s2a, s2b, p2a, p2b, fin, macc,
+    gh, bg, fw, dx, t2, vbuf, mixv, gqv, gkv,
+    lsem, fsem, osem, hsem, zs, zr, ws, wr, gs, gr, ms, mr, *scans,
 ):
     s, z, x, y, c = place()
     right, left = (z + 1) % 4, (z + 3) % 4
@@ -221,6 +231,17 @@
         copy = remote(*args)
         sends.append(copy)
         return copy
+
+    def load(src, dst, sem):
+        copy = pltpu.make_async_copy(src, dst, sem)
+        copy.start()
+        return copy
+
+    load_v = load(v_hbm, vbuf, lsem.at[2])
+    load_cot = load(cot_hbm, cot, lsem.at[0])
+    load_w = load(
+        w_hbm.at[pl.ds(pl.multiple_of(z * FEAT, FEAT), FEAT)], wt.at[SLOT[0]], lsem.at[1]
+    )
 
     barrier = pltpu.get_barrier_semaphore()
 
@@ -242,6 +263,8 @@
         signal(seq_of(z, y, c), z)
         signal(s, x)
 
+    spread(kt_ref, kx)
+    spread(qt_ref, qx)
     pl.semaphore_wait(barrier, len(known) + jnp.where(stays, 0, 2))
 
     row = c * 512 + x * 128 + y * 32
@@ -256,13 +279,38 @@
             s,
             there,
         )
-    edge = go(v_ref.at[pl.ds(ROWS - 16, 16)], halo, hsem.at[0], hsem.at[1], after, z)
-    load_cot = pltpu.make_async_copy(cot_hbm, cot, lsem.at[0])
-    load_cot.start()
-    load_w = pltpu.make_async_copy(
-        w_hbm.at[pl.ds(pl.multiple_of(z * FEAT, FEAT), FEAT)], wt.at[SLOT[0]], lsem.at[1]
-    )
-    load_w.start()
+    edge = go(v_hbm.at[pl.ds(ROWS - 16, 16)], halo, hsem.at[0], hsem.at[1], after, z)
+
+    cz = {}
+    for i, (lo, up) in enumerate(((0, 0), (128, 128))):
+        here = pl.ds(REST + lo, 128)
+        cz["l", i] = go(
+            cot_hbm.at[here], cf.at[2, pl.ds(lo, 128)], zs.at[18 + i], zr.at[18 + i], s, right
+        )
+        lo = 128 - lo
+        here = pl.ds(REST + lo, 128)
+        cz["r", i] = go(
+            cot_hbm.at[here], cf.at[0, pl.ds(lo, 128)], zs.at[20 + i], zr.at[20 + i], s, left
+        )
+    others = []
+    for k in (1, 2, 3):
+        for t in range(8):
+            at = pl.multiple_of((z + k) % 4 * FEAT + 128 * t, 128)
+            others.append(
+                load(
+                    w_hbm.at[pl.ds(at, 128)],
+                    pool.at[2 * (k - 1) + t // 4, t % 4],
+                    fsem.at[8 * (k - 1) + t],
+                )
+            )
+
+    def cot_on():
+        cz["l", 0].wait_recv()
+        a = pl.ds(0, 128)
+        cz["f", 0] = go(cf.at[2, a], cf.at[1, a], zs.at[22], zr.at[22], s, right)
+        cz["r", 0].wait_recv()
+        b = pl.ds(128, 128)
+        cz["f", 1] = go(cf.at[0, b], cf.at[1, b], zs.at[23], zr.at[23], s, left)
 
     def piece(group, px, py, half):
         at = pl.multiple_of(c * 512 + px * 128 + py * 32, 32)
@@ -307,10 +355,9 @@
         i = 33 + 31 * group
         w3[group] = go(half, half, ws.at[i], wr.at[i], sibling, z)
 
-    spread(kt_ref, kx)
-    spread(qt_ref, qx)
     w_first(0)
-    wide[8 : 8 + ROWS, :] = v_ref[...].astype(f32)
+    load_v.wait()
+    wide[8 : 8 + ROWS, :] = vbuf[...].astype(f32)
     w_first(1)
     edge.wait_recv()
     inside = jnp.where(s > 0, 1.0, 0.0).astype(f32)
@@ -327,6 +374,7 @@
     w_second(0)
     for n in (1, 2, 3):
         convolve(n)
+    cot_on()
     w_second(1)
     load_cot.wait()
 
@@ -353,19 +401,23 @@
     pair, along_y, along_x, back, done = scan_steps(scan_a, True)
     pair()
 
-    def fill(k, dst, lo, hi):
-        def part(b, carry):
-            rows = row_block(b)
+    def third(half, i):
+        return pl.ds(pl.multiple_of(half * HALF + i * (HALF // 2), HALF // 2), HALF // 2)
+
+    def fill(k, dst, half):
+        def part(i, carry):
+            rows = third(half, i)
             dst[rows, :] = nn(cot[rows, :], wt[SLOT[k]]).astype(bf16)
             return carry
 
-        lax.fori_loop(lo, hi, part, 0)
-
-    half_a, half_b = pl.ds(0, 512), pl.ds(512, 512)
+        lax.fori_loop(0, 2, part, 0)
+
+    half_a, half_b = pl.ds(0, HALF), pl.ds(HALF, HALF)
     rs = {}
     w3[0].wait_recv()
-    fill(2, opp, 0, 4)
+    fill(2, opp, 0)
     rs["or"] = go(opp.at[half_a], opp_l, zs.at[12], zr.at[12], s, right)
+    fill(2, opp, 1)
     rs["ol"] = go(opp.at[half_b], opp_r, zs.at[13], zr.at[13], s, left)
     w_third(1)
     along_y()
@@ -386,9 +438,9 @@
 
     lax.fori_loop(0, 2, intra, 0)
     w3[1].wait_recv()
-    fill(1, to_r, 2, 4)
+    fill(1, to_r, 1)
     rs["dr"] = go(to_r.at[half_b], from_l.at[half_b], zs.at[14], zr.at[14], s, right)
-    fill(3, to_l, 0, 2)
+    fill(3, to_l, 0)
     rs["dl"] = go(to_l.at[half_a], from_r.at[half_a], zs.at[15], zr.at[15], s, left)
     along_x()
     lax.fori_loop(2, 4, intra, 0)
@@ -412,10 +464,22 @@
 
     lax.fori_loop(0, NB, finish, 0)
 
-    def add_in(k, dst, got, lo):
-        def part(b, carry):
-            rows = row_block(lo + b)
-            here = row_block(b)
+    load_w.wait()
+    for copy in others:
+        copy.wait()
+    cz["l", 1].wait_recv()
+    cz["r", 1].wait_recv()
+    cz["f", 0].wait_recv()
+    cz["f", 1].wait_recv()
+    gf[...] = nn(cot[REST:ROWS, :], wt[SLOT[0]])
+    for k in (1, 2, 3):
+        for t in (0, 1):
+            block = pool[2 * (k - 1) + t].reshape(512, CH)
+            gf[...] += nn(cf[k - 1, :, 512 * t : 512 * t + 512], block)
+
+    def add_in(k, dst, got, half):
+        def part(i, carry):
+            rows, here = third(half, i), third(0, i)
             term = nn(cot[rows, :], wt[SLOT[k]]) + got[here, :].astype(f32)
             dst[rows, :] = term.astype(bf16)
             return carry
@@ -426,7 +490,7 @@
     add_in(1, to_r, opp_l, 0)
     rs["ar"] = go(to_r.at[half_a], from_l.at[half_a], zs.at[16], zr.at[16], s, right)
     rs["ol"].wait_recv()
-    add_in(3, to_l, opp_r, 2)
+    add_in(3, to_l, opp_r, 1)
     rs["al"] = go(to_l.at[half_b], from_r.at[half_b], zs.at[17], zr.at[17], s, left)
 
     ag = {}
@@ -442,78 +506,107 @@
         ag["r", e].wait_recv()
         ag["f", e] = go(oall.at[1, e], oall.at[2, e], zs.at[8 + e], zr.at[8 + e], s, left)
 
-    def four(k, rows):
-        return jnp.concatenate([oall[k, h, rows, :] for h in range(HEADS)], axis=1)
+    def joined(k, rows, heads):
+        return jnp.concatenate([oall[k, h, rows, :] for h in heads], axis=1)
 
     g1, g2, g3, g4 = {}, {}, {}, {}
-
-    def gw_term(k):
+    sem0 = {name: 16 * i for i, name in enumerate(UNITS)}
+
+    def gw_term(u, split=False):
+        k, heads, off, w = UNITS[u]
+        cols = pl.ds(2 * off, 2 * w)
+        i = sem0[u]
+
         def part(t, carry):
-            term = nn(cott[row_block(t), :], four(k, slice(None))).astype(bf16)
-            gwp[0, k, t] = term[0:128]
-            gwp[1, k, t] = term[128:256]
+            term = nn(cott[row_block(t), :], joined(k, slice(None), heads)).astype(bf16)
+            pool[k, t, :, cols] = term[0:128]
+            pool[4 + k, t, :, cols] = term[128:256]
             return carry
 
+        if split:
+            g1[u] = []
+            for t in range(4):
+                part(t, 0)
+                g1[u].append(
+                    go(
+                        pool.at[4 * (1 - c) + k, t, :, cols],
+                        r1.at[k, t, :, cols], gs.at[i + t], gr.at[i + t], sibling, z,
+                    )
+                )
+        else:
+            lax.fori_loop(0, 4, part, 0)
+            theirs = pool.at[4 * (1 - c) + k, :, :, cols]
+            g1[u] = [go(theirs, r1.at[k, :, :, cols], gs.at[i], gr.at[i], sibling, z)]
+
+    def gw_first(u):
+        k, heads, off, w = UNITS[u]
+        cols = slice(2 * off, 2 * off + 2 * w)
+        for copy in g1[u]:
+            copy.wait_recv()
+
+        def part(t, carry):
+            both = pool[4 * c + k, t, :, cols].astype(f32) + r1[k, t, :, cols].astype(f32)
+            gsum[k, t, :, cols] = both.astype(bf16)
+            return carry
+
         lax.fori_loop(0, 4, part, 0)
-        g1[k] = go(gwp.at[1 - c, k], r1.at[k], gs.at[k], gr.at[k], sibling, z)
-
-    def gw_first(k):
-        g1[k].wait_recv()
-
-        def part(t, carry):
-            gsum[k, t] = (gwp[c, k, t].astype(f32) + r1[k, t].astype(f32)).astype(bf16)
-            return carry
-
-        lax.fori_loop(0, 4, part, 0)
-        for j in (1, 2, 3):
+        for j in (2, 1, 3):
             nx, ny = (x + j) % 4, (y + j) % 4
-            i = 4 + 12 * k + j - 1
+            i = sem0[u] + 4 + j - 1
             rows = pl.ds(pl.multiple_of(nx * 32, 32), 32)
-            g2[k, 0, j] = go(
-                gsum.at[k, :, rows, pl.ds(0, 256)],
-                p1a.at[k, j - 1], gs.at[i], gr.at[i], seq_of(nx, y, c), z,
+            g2[u, 0, j] = go(
+                gsum.at[k, :, rows, pl.ds(2 * off, w)],
+                p1a.at[k, j - 1, :, :, pl.ds(off, w)], gs.at[i], gr.at[i], seq_of(nx, y, c), z,
             )
             i += 3
-            g2[k, 1, j] = go(
-                gsum.at[k, ny, :, pl.ds(256, 256)],
-                p1b.at[k, j - 1], gs.at[i], gr.at[i], seq_of(x, ny, c), z,
+            g2[u, 1, j] = go(
+                gsum.at[k, ny, :, pl.ds(2 * off + w, w)],
+                p1b.at[k, j - 1, :, pl.ds(off, w)], gs.at[i], gr.at[i], seq_of(x, ny, c), z,
             )
 
     my_rows = pl.ds(pl.multiple_of(x * 32, 32), 32)
 
-    def gw_second(k):
-        sum_a = gsum[k, :, my_rows, 0:256].astype(f32)
-        sum_b = gsum[k, y, :, 256:512].astype(f32)
+    def gw_second(u):
+        k, heads, off, w = UNITS[u]
+        cols = slice(off, off + w)
+        sum_a = gsum[k, :, my_rows, 2 * off : 2 * off + w].astype(f32)
+        sum_b = gsum[k, y, :, 2 * off + w : 2 * off + 2 * w].astype(f32)
         for j in (1, 3, 2):
-            g2[k, 0, j].wait_recv()
-            sum_a = sum_a + p1a[k, j - 1].astype(f32)
-            g2[k, 1, j].wait_recv()
-            sum_b = sum_b + p1b[k, j - 1].astype(f32)
-        s2a[k] = sum_a.astype(bf16)
-        s2b[k] = sum_b.astype(bf16)
-        for j in (1, 2, 3):
+            g2[u, 0, j].wait_recv()
+            sum_a = sum_a + p1a[k, j - 1, :, :, cols].astype(f32)
+            g2[u, 1, j].wait_recv()
+            sum_b = sum_b + p1b[k, j - 1, :, cols].astype(f32)
+        s2a[k, :, :, cols] = sum_a.astype(bf16)
+        s2b[k, :, cols] = sum_b.astype(bf16)
+        for j in (2, 1, 3):
             nx, ny = (x + j) % 4, (y + j) % 4
-            i = 4 + 12 * k + 6 + j - 1
+            i = sem0[u] + 10 + j - 1
             rows = pl.ds(pl.multiple_of(nx * 32, 32), 32)
-            g3[k, 0, j] = go(
-                s2a.at[k, ny], p2a.at[k, j - 1], gs.at[i], gr.at[i], seq_of(x, ny, c), z
+            here = pl.ds(off, w)
+            g3[u, 0, j] = go(
+                s2a.at[k, ny, :, here],
+                p2a.at[k, j - 1, :, here], gs.at[i], gr.at[i], seq_of(x, ny, c), z,
             )
             i += 3
-            g3[k, 1, j] = go(
-                s2b.at[k, rows], p2b.at[k, j - 1], gs.at[i], gr.at[i], seq_of(nx, y, c), z
+            g3[u, 1, j] = go(
+                s2b.at[k, rows, here],
+                p2b.at[k, j - 1, :, here], gs.at[i], gr.at[i], seq_of(nx, y, c), z,
             )
 
-    def gw_third(k):
-        sum_a = s2a[k, y].astype(f32)
-        sum_b = s2b[k, my_rows, :].astype(f32)
+    def gw_third(u):
+        k, heads, off, w = UNITS[u]
+        cols = slice(off, off + w)
+        sum_a = s2a[k, y, :, cols].astype(f32)
+        sum_b = s2b[k, my_rows, cols].astype(f32)
         for j in (1, 3, 2):
-            g3[k, 0, j].wait_recv()
-            sum_a = sum_a + p2a[k, j - 1].astype(f32)
-            g3[k, 1, j].wait_recv()
-            sum_b = sum_b + p2b[k, j - 1].astype(f32)
-        fin[k, :, 0:256] = sum_a.astype(bf16)
-        fin[k, :, 256:512] = sum_b.astype(bf16)
-
+            g3[u, 0, j].wait_recv()
+            sum_a = sum_a + p2a[k, j - 1, :, cols].astype(f32)
+            g3[u, 1, j].wait_recv()
+            sum_b = sum_b + p2b[k, j - 1, :, cols].astype(f32)
+        fin[k, :, cols] = sum_a.astype(bf16)
+        fin[k, :, 256 + off : 256 + off + w] = sum_b.astype(bf16)
+
+    def gw_move(k):
         def move():
             return pltpu.make_async_remote_copy(
                 src_ref=fin.at[k],
@@ -554,37 +647,48 @@
                     device_id_type=pl.DeviceIdType.MESH,
                 ).wait_recv()
 
-    def mix(ks, first, last):
+    out_copies = []
+
+    def mix(parts, first, last):
         def part(b, carry):
             rows = row_block(b)
             for u in (0, 1):
                 cols = slice(512 * u, 512 * u + 512)
                 acc = None if first else macc[rows, cols]
-                for k in ks:
-                    term = nt(four(k, rows), wt[SLOT[k], cols, :])
+                for k, heads in parts:
+                    if len(heads) == HEADS:
+                        rhs = wt[SLOT[k], cols, :]
+                    else:
+                        lanes = [slice(h * DV, (h + 1) * DV) for h in heads]
+                        rhs = jnp.concatenate([wt[SLOT[k], cols, o] for o in lanes], axis=1)
+                    term = nt(joined(k, rows, heads), rhs)
                     acc = term if acc is None else acc + term
                 if last:
-                    mixed_ref[rows, cols] = acc.astype(bf16)
+                    mixv[rows, cols] = acc.astype(bf16)
                 else:
                     macc[rows, cols] = acc
+            if last:
+                pltpu.make_async_copy(mixv.at[rows], mixed_hbm.at[rows], osem.at[b]).start()
             return carry
 
         lax.fori_loop(0, NB, part, 0)
-
-    gw_term(0)
-    load_w.wait()
-    mix((0,), True, False)
-    gw_first(0)
-
-    for name in ("dr", "dl", "ar", "al"):
-        rs[name].wait_recv()
+        if last:
+            for b in range(NB):
+                rows = pl.ds(b * BLOCK, BLOCK)
+                out_copies.append(
+                    pltpu.make_async_copy(mixv.at[rows], mixed_hbm.at[rows], osem.at[b])
+                )
+
+    every = (0, 1, 2, 3)
+    gw_term("0")
+    mix(((0, every),), True, False)
+    gw_first("0")
+
     tot_b, ent_b = scan_b[0], scan_b[9]
     tot_b[...] = jnp.zeros_like(tot_b)
 
-    def back_states(n, carry):
+    def back_states(n, grad_out):
         rows = row_block(n)
-        grad_out = nn(cot[rows, :], wt[SLOT[0]])
-        grad_out = grad_out + from_r[rows, :].astype(f32) + from_l[rows, :].astype(f32)
         for h in range(HEADS):
             lanes = slice(h * DV, (h + 1) * DV)
             hidden = hid[rows, lanes]
@@ -597,9 +701,18 @@
             own = nn(phi(qx, h, rows), grad)
             bg[n, h] = own
             tot_b[h] += own
+
+    def back_rest(n, carry):
+        rows = row_block(n)
+        grad_out = nn(cot[rows, :], wt[SLOT[0]])
+        grad_out = grad_out + from_r[rows, :].astype(f32) + from_l[rows, :].astype(f32)
+        back_states(n, grad_out)
         return carry
 
-    lax.fori_loop(0, NB, back_states, 0)
+    back_states(NB - 1, gf[...])
+    for name in ("dr", "dl", "ar", "al"):
+        rs[name].wait_recv()
+    lax.fori_loop(0, NB - 1, back_rest, 0)
     pair, along_y, along_x, back, done = scan_steps(scan_b, False)
 
     def back_intra(n, carry):
@@ -616,7 +729,7 @@
             att = jnp.where(mask_t, 1.0 + sc * (0.25 + sc * (1.0 / 32)), 0.0).astype(bf16)
             wide[rows, lanes] = nn(att, g)
             across = phi_back(nt(prev[n, h], g), qx, t2, h, rows)
-            gq_ref[entries, rows] = (nn(kh, ds) + across).astype(bf16)
+            gqv[entries, rows] = (nn(kh, ds) + across).astype(bf16)
             dx[entries, rows] = nt(qh, ds)
         return carry
 
@@ -629,7 +742,8 @@
     hand_on(1)
     lax.fori_loop(3, 4, back_intra, 0)
     back()
-    gw_second(0)
+    gw_second("0")
+    out_copies.append(load(gqv, gq_hbm, osem.at[4]))
     done()
 
     def suffix(t, carry):
@@ -649,7 +763,7 @@
             entries = slice(16 * h, 16 * h + 16)
             wide[rows, lanes] += tn(phi(kx, h, rows), fw[n, h])
             across = phi_back(nt(fw[n, h], conv[rows, lanes]), kx, t2, h, rows)
-            gk_ref[entries, rows] = (dx[entries, rows] + across).astype(bf16)
+            gkv[entries, rows] = (dx[entries, rows] + across).astype(bf16)
         return carry
 
     lax.fori_loop(0, 1, back_finish, 0)
@@ -664,32 +778,80 @@
         acc = cw_ref[0:1, :] * wide[at : at + BLOCK, :]
         for j in (1, 2):
             acc = acc + cw_ref[j : j + 1, :] * wide[at + j : at + j + BLOCK, :]
-        gv_ref[at : at + BLOCK, :] = acc.astype(bf16)
-
-    gw_third(0)
+        vbuf[at : at + BLOCK, :] = acc.astype(bf16)
+    out_copies.append(load(gkv, gk_hbm, osem.at[5]))
+    out_copies.append(load(vbuf, gv_hbm, osem.at[6]))
+
+    gw_third("0")
+    gw_move(0)
     ag["l", 2].wait_recv()
     ag["l", 3].wait_recv()
-    gw_term(3)
+    gw_term("3")
     ag["r", 0].wait_recv()
     ag["r", 1].wait_recv()
-    gw_term(1)
-    gw_first(3)
-    gw_first(1)
-    mix((1, 3), False, False)
-    gw_second(3)
-    gw_second(1)
-    for h in range(HEADS):
-        ag["f", h].wait_recv()
-    gw_term(2)
-    gw_third(3)
-    gw_third(1)
-    gw_first(2)
-    mix((2,), False, True)
-    gw_second(2)
-    gw_third(2)
+    gw_term("1")
+    gw_first("3")
+    gw_first("1")
+    mix(((1, every), (3, every)), False, False)
+    gw_second("3")
+    gw_second("1")
+    ag["f", 0].wait_recv()
+    ag["f", 2].wait_recv()
+    gw_term("2a")
+    mix(((2, (0, 2)),), False, False)
+    gw_first("2a")
+    gw_third("3")
+    gw_move(3)
+    gw_third("1")
+    gw_move(1)
+    ag["f", 1].wait_recv()
+    ag["f", 3].wait_recv()
+    gw_term("2b", True)
+    gw_second("2a")
+    gw_first("2b")
+    mix(((2, (1, 3)),), False, True)
+    gw_third("2a")
+    gw_second("2b")
+    gw_third("2b")
+    gw_move(2)
+    for copy in out_copies:
+        copy.wait()
     gw_done()
     for copy in sends:
         copy.wait_send()
+
+
+def hand_over_kernel(*refs):
+    arrays, results, held, sem_in, sem_out = refs[:5], refs[5:10], refs[10:15], refs[15], refs[16]
+    first, second = [], []
+    for src, mid, dst in zip(arrays, held, results, strict=True):
+        rows = max(src.shape[0] // 4, 32)
+        for at in range(0, src.shape[0], rows):
+            part = pl.ds(at, rows)
+            i = len(first)
+            first.append(pltpu.make_async_copy(src.at[part], mid.at[part], sem_in.at[i]))
+            second.append(pltpu.make_async_copy(mid.at[part], dst.at[part], sem_out.at[i]))
+    for copy in first:
+        copy.start()
+    for copy, onward in zip(first, second, strict=True):
+        copy.wait()
+        onward.start()
+    for copy in second:
+        copy.wait()
+
+
+def hand_over(*arrays):
+    hbm = pl.BlockSpec(memory_space=pl.ANY)
+    return pl.pallas_call(
+        hand_over_kernel,
+        out_shape=tuple(jax.ShapeDtypeStruct(a.shape, a.dtype) for a in arrays),
+        in_specs=[hbm] * 5,
+        out_specs=(hbm,) * 5,
+        scratch_shapes=[pltpu.VMEM(a.shape, a.dtype) for a in arrays]
+        + [pltpu.SemaphoreType.DMA((20,))] * 2,
+        compiler_params=pltpu.CompilerParams(vmem_limit_bytes=VMEM_LIMIT),
+        name="hand_over",
+    )(*arrays)
 
 
 def on_device(query, key_feat, values, conv_w, gain, w_out, cotangent):
@@ -706,8 +868,8 @@
             jax.ShapeDtypeStruct((ROWS, CH), bf16),
             jax.ShapeDtypeStruct((128, CH), bf16),
         ),
-        in_specs=[vm] * 5 + [hbm] * 2,
-        out_specs=(vm,) * 5,
+        in_specs=[vm] * 4 + [hbm] * 3,
+        out_specs=(hbm,) * 4 + (vm,),
         scratch_shapes=[
             vmem((16, CH), bf16),
             vmem((8, CH), f32),
@@ -723,14 +885,16 @@
             vmem((4, FEAT, CH), bf16),
             vmem((ROWS, FEAT), bf16),
             vmem((FEAT, ROWS), bf16),
-            vmem((ROWS, CH), bf16),
-            vmem((ROWS, CH), bf16),
-            vmem((ROWS, CH), bf16),
-            vmem((512, CH), bf16),
-            vmem((512, CH), bf16),
-            vmem((ROWS, CH), bf16),
-            vmem((ROWS, CH), bf16),
-            vmem((2, 4, 4, 128, CH), bf16),
+            vmem((REST, CH), bf16),
+            vmem((REST, CH), bf16),
+            vmem((REST, CH), bf16),
+            vmem((HALF, CH), bf16),
+            vmem((HALF, CH), bf16),
+            vmem((REST, CH), bf16),
+            vmem((REST, CH), bf16),
+            vmem((3, FILL, FEAT), bf16),
+            vmem((FILL, CH), f32),
+            vmem((8, 4, 128, CH), bf16),
             vmem((4, 4, 128, CH), bf16),
             vmem((4, 4, 128, CH), bf16),
             vmem((4, 3, 4, 32, 256), bf16),
@@ -746,14 +910,20 @@
             vmem((NB, HEADS, NF, DV), bf16),
             vmem((HEADS * FD, ROWS), f32),
             vmem((7, 32, BLOCK), f32),
-            dma((2,)),
+            vmem((ROWS, CH), bf16),
+            vmem((ROWS, FEAT), bf16),
+            vmem((HEADS * FD, ROWS), bf16),
+            vmem((HEADS * FD, ROWS), bf16),
+            dma((3,)),
+            dma((24,)),
+            dma((7,)),
             dma((4,)),
-            dma((18,)),
-            dma((18,)),
+            dma((24,)),
+            dma((24,)),
             dma((65,)),
             dma((65,)),
-            dma((52,)),
-            dma((52,)),
+            dma((80,)),
+            dma((80,)),
             dma((4,)),
             dma((4,)),
         ]
@@ -762,7 +932,8 @@
             collective_id=0, has_side_effects=True, vmem_limit_bytes=VMEM_LIMIT
         ),
         name="sublayer",
-    )(query.T, key_feat.T, values, conv_w, gain.reshape(1, CH), w_out, cotangent)
+    )(query.T, key_feat.T, conv_w, gain.reshape(1, CH), values, w_out, cotangent)
+    mixed, gq, gk, gv, gw = hand_over(mixed, gq, gk, gv, gw)
     return mixed, gq.T, gk.T, gv, gw
 
 

time: 127 us -> 117 us (0.921)
  local copies, waits for them, and re-layouts: 6.13 us -> 0 us
  Pallas kernels: 119 us -> 116 us
    pallas_call x1, Pallas kernels: 119 us -> 113 us  [on_device(): pl.pallas_call(kernel, out_shape=(jax.ShapeDtypeStruct((ROWS, FEAT), bf16...]
    unnamed x13 -> x0, local copies, waits for them, and re-layouts: 6.13 us -> none
    pallas_call x0 -> x1, Pallas kernels: none -> 3.16 us  [hand_over(): pl.pallas_call(hand_over_kernel, out_shape=tuple((jax.ShapeDtypeStruct(a....]
where the time goes in v3:
time: 117 us
  Pallas kernels  116 us (99%)
    pallas_call x1, Pallas kernels, on_device(): pl.pallas_call(kernel, out_shape=(jax.ShapeDtypeStruct((ROWS, FEAT), bf16...  113 us
    pallas_call x1, Pallas kernels, hand_over(): pl.pallas_call(hand_over_kernel, out_shape=tuple((jax.ShapeDtypeStruct(a....  3.16 us

profile of v3, /device:TPU:4, one launch (start us, length us, event | category | flops | bytes accessed | tf_op | source)
XLA Modules:
  0.0 116.9 jit_solution(6317140243353941772)
XLA Ops:
  0.6 113.0 %sublayer.1 = (bf16[1024,1024]{1,0:T(8,128)(2,1)}, bf16[64,1024]{1,0:T(8,128)(2,1)}, bf16[64,1024]{1,0:T(8,128)(2,1)}, bf16[1024,512]{1,0:T(8,128)(2,1)}, bf16[128,512]{1,0:T(8,128)(2,1)}) custom-call(bf16[64,1024]{1,0:T(8,128)(2,1)} %bitcast.5, bf16[64,1024]{1,0:T(8,128)(2,1)} %bitcast.6, f32[3,512]{1,0:T(4,128)} %cw_ref.1, f32[1,512]{1,0:T(1,128)} %bitcast.7, ...), custom_call_target="tpu_custom_call" | custom-call | tf_op jit(solution)/shard_map/sublayer/pallas_call | solution.py:862
  113.6 3.2 %hand_over.1 = (bf16[1024,1024]{1,0:T(8,128)(2,1)}, bf16[64,1024]{1,0:T(8,128)(2,1)}, bf16[64,1024]{1,0:T(8,128)(2,1)}, bf16[1024,512]{1,0:T(8,128)(2,1)}, bf16[128,512]{1,0:T(8,128)(2,1)}) custom-call(bf16[1024,1024]{1,0:T(8,128)(2,1)} %get-tuple-element.15.refs_0_, bf16[64,1024]{1,0:T(8,128)(2,1)} %get-tuple-element.16.refs_1_, ...), custom_call_target="tpu_custom_call" | custom-call | tf_op jit(solution)/shard_map/hand_over/pallas_call | solution.py:845

commit v4 on v3

--- a/solution.py
+++ b/solution.py
@@ -649,7 +649,7 @@
 
     out_copies = []
 
-    def mix(parts, first, last):
+    def mix(parts, first, last, lo=0, hi=NB):
         def part(b, carry):
             rows = row_block(b)
             for u in (0, 1):
@@ -671,9 +671,9 @@
                 pltpu.make_async_copy(mixv.at[rows], mixed_hbm.at[rows], osem.at[b]).start()
             return carry
 
-        lax.fori_loop(0, NB, part, 0)
+        lax.fori_loop(lo, hi, part, 0)
         if last:
-            for b in range(NB):
+            for b in range(lo, hi):
                 rows = pl.ds(b * BLOCK, BLOCK)
                 out_copies.append(
                     pltpu.make_async_copy(mixv.at[rows], mixed_hbm.at[rows], osem.at[b])
@@ -792,26 +792,26 @@
     gw_term("1")
     gw_first("3")
     gw_first("1")
+    ag["f", 0].wait_recv()
+    ag["f", 2].wait_recv()
+    gw_term("2a")
     mix(((1, every), (3, every)), False, False)
     gw_second("3")
     gw_second("1")
-    ag["f", 0].wait_recv()
-    ag["f", 2].wait_recv()
-    gw_term("2a")
-    mix(((2, (0, 2)),), False, False)
     gw_first("2a")
+    ag["f", 1].wait_recv()
+    ag["f", 3].wait_recv()
+    gw_term("2b", True)
+    mix(((2, every),), False, True, 0, 2)
+    gw_first("2b")
+    mix(((2, every),), False, True, 2, 4)
+    gw_second("2a")
     gw_third("3")
     gw_move(3)
     gw_third("1")
     gw_move(1)
-    ag["f", 1].wait_recv()
-    ag["f", 3].wait_recv()
-    gw_term("2b", True)
-    gw_second("2a")
-    gw_first("2b")
-    mix(((2, (1, 3)),), False, True)
+    gw_second("2b")
     gw_third("2a")
-    gw_second("2b")
     gw_third("2b")
     gw_move(2)
     for copy in out_copies:

time: 117 us -> 113 us (0.966)
  Pallas kernels: 116 us -> 112 us
    pallas_call x1, Pallas kernels: 113 us -> 109 us  [on_device(): pl.pallas_call(kernel, out_shape=(jax.ShapeDtypeStruct((ROWS, FEAT), bf16...]
where the time goes in v4:
time: 113 us
  Pallas kernels  112 us (99%)
    pallas_call x1, Pallas kernels, on_device(): pl.pallas_call(kernel, out_shape=(jax.ShapeDtypeStruct((ROWS, FEAT), bf16...  109 us
    pallas_call x1, Pallas kernels, hand_over(): pl.pallas_call(hand_over_kernel, out_shape=tuple((jax.ShapeDtypeStruct(a....  3.16 us

profile of v4, /device:TPU:4, one launch (start us, length us, event | category | flops | bytes accessed | tf_op | source)
XLA Modules:
  0.0 113.1 jit_solution(16955947970000108449)
XLA Ops:
  0.6 109.1 %sublayer.1 = (bf16[1024,1024]{1,0:T(8,128)(2,1)}, bf16[64,1024]{1,0:T(8,128)(2,1)}, bf16[64,1024]{1,0:T(8,128)(2,1)}, bf16[1024,512]{1,0:T(8,128)(2,1)}, bf16[128,512]{1,0:T(8,128)(2,1)}) custom-call(bf16[64,1024]{1,0:T(8,128)(2,1)} %bitcast.5, bf16[64,1024]{1,0:T(8,128)(2,1)} %bitcast.6, f32[3,512]{1,0:T(4,128)} %cw_ref.1, f32[1,512]{1,0:T(1,128)} %bitcast.7, ...), custom_call_target="tpu_custom_call" | custom-call | tf_op jit(solution)/shard_map/sublayer/pallas_call | solution.py:862
  109.8 3.2 %hand_over.1 = (bf16[1024,1024]{1,0:T(8,128)(2,1)}, bf16[64,1024]{1,0:T(8,128)(2,1)}, bf16[64,1024]{1,0:T(8,128)(2,1)}, bf16[1024,512]{1,0:T(8,128)(2,1)}, bf16[128,512]{1,0:T(8,128)(2,1)}) custom-call(bf16[1024,1024]{1,0:T(8,128)(2,1)} %get-tuple-element.15.refs_0_, bf16[64,1024]{1,0:T(8,128)(2,1)} %get-tuple-element.16.refs_1_, ...), custom_call_target="tpu_custom_call" | custom-call | tf_op jit(solution)/shard_map/hand_over/pallas_call | solution.py:845

commit v5 on v4

--- a/solution.py
+++ b/solution.py
@@ -213,12 +213,12 @@
 
 
 def kernel(
-    qt_ref, kt_ref, cw_ref, gain_ref, v_hbm, w_hbm, cot_hbm,
-    mixed_hbm, gq_hbm, gk_hbm, gv_hbm, gw_ref,
+    qt_hbm, kt_hbm, cw_hbm, gain_hbm, v_hbm, w_hbm, cot_hbm,
+    mixed_hbm, gq_hbm, gk_hbm, gv_hbm, gw_hbm,
     halo, halo_back, edge_rows, wide, qx, kx, conv, st, hid, prev, oall,
     wt, cot, cott, opp, to_r, to_l, opp_l, opp_r, from_r, from_l, cf, gf,
     pool, r1, gsum, p1a, p1b, s2a, s2b, p2a, p2b, fin, macc,
-    gh, bg, fw, dx, t2, vbuf, mixv, gqv, gkv,
+    gh, bg, fw, dx, t2, vbuf, mixv, gqv, gkv, qt_ref, kt_ref, cw_ref, gain_ref,
     lsem, fsem, osem, hsem, zs, zr, ws, wr, gs, gr, ms, mr, *scans,
 ):
     s, z, x, y, c = place()
@@ -237,6 +237,12 @@
         copy.start()
         return copy
 
+    small = [
+        load(src, dst, lsem.at[3 + i])
+        for i, (src, dst) in enumerate(
+            ((kt_hbm, kt_ref), (qt_hbm, qt_ref), (cw_hbm, cw_ref), (gain_hbm, gain_ref))
+        )
+    ]
     load_v = load(v_hbm, vbuf, lsem.at[2])
     load_cot = load(cot_hbm, cot, lsem.at[0])
     load_w = load(
@@ -263,6 +269,8 @@
         signal(seq_of(z, y, c), z)
         signal(s, x)
 
+    for copy in small:
+        copy.wait()
     spread(kt_ref, kx)
     spread(qt_ref, qx)
     pl.semaphore_wait(barrier, len(known) + jnp.where(stays, 0, 2))
@@ -610,7 +618,7 @@
         def move():
             return pltpu.make_async_remote_copy(
                 src_ref=fin.at[k],
-                dst_ref=gw_ref.at[my_rows],
+                dst_ref=gw_hbm.at[my_rows],
                 send_sem=ms.at[k],
                 recv_sem=mr.at[x],
                 device_id={"seq": seq_of(z, y, c), "head": (z + k) % 4},
@@ -624,7 +632,7 @@
 
             @pl.when(stays)
             def _():
-                gw_ref[my_rows, :] = fin[0]
+                load(fin.at[0], gw_hbm.at[my_rows], ms.at[0]).wait()
 
             @pl.when(jnp.logical_not(stays))
             def _():
@@ -640,7 +648,7 @@
             def _():
                 pltpu.make_async_remote_copy(
                     src_ref=fin.at[0],
-                    dst_ref=gw_ref.at[pl.ds(32 * xs, 32)],
+                    dst_ref=gw_hbm.at[pl.ds(32 * xs, 32)],
                     send_sem=ms.at[0],
                     recv_sem=mr.at[xs],
                     device_id={"seq": seq_of(z, y, c), "head": (z + 1) % 4},
@@ -825,7 +833,7 @@
     arrays, results, held, sem_in, sem_out = refs[:5], refs[5:10], refs[10:15], refs[15], refs[16]
     first, second = [], []
     for src, mid, dst in zip(arrays, held, results, strict=True):
-        rows = max(src.shape[0] // 4, 32)
+        rows = max(src.shape[0] // 8, 32)
         for at in range(0, src.shape[0], rows):
             part = pl.ds(at, rows)
             i = len(first)
@@ -848,14 +856,13 @@
         in_specs=[hbm] * 5,
         out_specs=(hbm,) * 5,
         scratch_shapes=[pltpu.VMEM(a.shape, a.dtype) for a in arrays]
-        + [pltpu.SemaphoreType.DMA((20,))] * 2,
+        + [pltpu.SemaphoreType.DMA((24,))] * 2,
         compiler_params=pltpu.CompilerParams(vmem_limit_bytes=VMEM_LIMIT),
         name="hand_over",
     )(*arrays)
 
 
 def on_device(query, key_feat, values, conv_w, gain, w_out, cotangent):
-    vm = pl.BlockSpec(memory_space=pltpu.VMEM)
     hbm = pl.BlockSpec(memory_space=pl.ANY)
     dma = pltpu.SemaphoreType.DMA
     vmem = pltpu.VMEM
@@ -868,8 +875,8 @@
             jax.ShapeDtypeStruct((ROWS, CH), bf16),
             jax.ShapeDtypeStruct((128, CH), bf16),
         ),
-        in_specs=[vm] * 4 + [hbm] * 3,
-        out_specs=(hbm,) * 4 + (vm,),
+        in_specs=[hbm] * 7,
+        out_specs=(hbm,) * 5,
         scratch_shapes=[
             vmem((16, CH), bf16),
             vmem((8, CH), f32),
@@ -914,7 +921,11 @@
             vmem((ROWS, FEAT), bf16),
             vmem((HEADS * FD, ROWS), bf16),
             vmem((HEADS * FD, ROWS), bf16),
-            dma((3,)),
+            vmem((HEADS * FD, ROWS), bf16),
+            vmem((HEADS * FD, ROWS), bf16),
+            vmem((3, CH), f32),
+            vmem((1, CH), f32),
+            dma((7,)),
             dma((24,)),
             dma((7,)),
             dma((4,)),

time: 113 us -> 112 us (level)
    pallas_call x1, Pallas kernels: 109 us -> 108 us  [on_device(): pl.pallas_call(kernel, out_shape=(jax.ShapeDtypeStruct((ROWS, FEAT), bf16...]
where the time goes in v5:
time: 112 us
  Pallas kernels  111 us (99%)
    pallas_call x1, Pallas kernels, on_device(): pl.pallas_call(kernel, out_shape=(jax.ShapeDtypeStruct((ROWS, FEAT), bf16...  108 us
    pallas_call x1, Pallas kernels, hand_over(): pl.pallas_call(hand_over_kernel, out_shape=tuple((jax.ShapeDtypeStruct(a....  3.14 us

profile of v5, /device:TPU:4, one launch (start us, length us, event | category | flops | bytes accessed | tf_op | source)
XLA Modules:
  0.0 111.8 jit_solution(8311804704961462527)
XLA Ops:
  0.6 107.8 %sublayer.1 = (bf16[1024,1024]{1,0:T(8,128)(2,1)}, bf16[64,1024]{1,0:T(8,128)(2,1)}, bf16[64,1024]{1,0:T(8,128)(2,1)}, bf16[1024,512]{1,0:T(8,128)(2,1)}, bf16[128,512]{1,0:T(8,128)(2,1)}) custom-call(bf16[64,1024]{1,0:T(8,128)(2,1)} %bitcast.5, bf16[64,1024]{1,0:T(8,128)(2,1)} %bitcast.6, f32[3,512]{1,0:T(4,128)} %cw_hbm.1, f32[1,512]{1,0:T(1,128)} %bitcast.7, ...), custom_call_target="tpu_custom_call" | custom-call | tf_op jit(solution)/shard_map/sublayer/pallas_call | solution.py:869
  108.5 3.1 %hand_over.1 = (bf16[1024,1024]{1,0:T(8,128)(2,1)}, bf16[64,1024]{1,0:T(8,128)(2,1)}, bf16[64,1024]{1,0:T(8,128)(2,1)}, bf16[1024,512]{1,0:T(8,128)(2,1)}, bf16[128,512]{1,0:T(8,128)(2,1)}) custom-call(bf16[1024,1024]{1,0:T(8,128)(2,1)} %get-tuple-element.15.refs_0_, bf16[64,1024]{1,0:T(8,128)(2,1)} %get-tuple-element.16.refs_1_, ...), custom_call_target="tpu_custom_call" | custom-call | tf_op jit(solution)/shard_map/hand_over/pallas_call | solution.py:853

commit v6 on v5

--- a/solution.py
+++ b/solution.py
@@ -196,9 +196,10 @@
 
 SLOT = {2: 0, 1: 1, 3: 2, 0: 3}
 GROUPS = ((2,), (1, 3))
-FILL = 256
+FILL = 192
 REST = ROWS - FILL
 HALF = REST // 2
+PART = FILL // 2
 UNITS = {
     "0": (0, (0, 1, 2, 3), 0, 256),
     "1": (1, (0, 1, 2, 3), 0, 256),
@@ -290,15 +291,15 @@
     edge = go(v_hbm.at[pl.ds(ROWS - 16, 16)], halo, hsem.at[0], hsem.at[1], after, z)
 
     cz = {}
-    for i, (lo, up) in enumerate(((0, 0), (128, 128))):
-        here = pl.ds(REST + lo, 128)
+    for i, lo in enumerate((0, PART)):
+        here = pl.ds(REST + lo, PART)
         cz["l", i] = go(
-            cot_hbm.at[here], cf.at[2, pl.ds(lo, 128)], zs.at[18 + i], zr.at[18 + i], s, right
+            cot_hbm.at[here], cf.at[2, pl.ds(lo, PART)], zs.at[18 + i], zr.at[18 + i], s, right
         )
-        lo = 128 - lo
-        here = pl.ds(REST + lo, 128)
+        lo = PART - lo
+        here = pl.ds(REST + lo, PART)
         cz["r", i] = go(
-            cot_hbm.at[here], cf.at[0, pl.ds(lo, 128)], zs.at[20 + i], zr.at[20 + i], s, left
+            cot_hbm.at[here], cf.at[0, pl.ds(lo, PART)], zs.at[20 + i], zr.at[20 + i], s, left
         )
     others = []
     for k in (1, 2, 3):
@@ -314,10 +315,10 @@
 
     def cot_on():
         cz["l", 0].wait_recv()
-        a = pl.ds(0, 128)
+        a = pl.ds(0, PART)
         cz["f", 0] = go(cf.at[2, a], cf.at[1, a], zs.at[22], zr.at[22], s, right)
         cz["r", 0].wait_recv()
-        b = pl.ds(128, 128)
+        b = pl.ds(PART, PART)
         cz["f", 1] = go(cf.at[0, b], cf.at[1, b], zs.at[23], zr.at[23], s, left)
 
     def piece(group, px, py, half):
@@ -383,15 +384,9 @@
     for n in (1, 2, 3):
         convolve(n)
     cot_on()
+    w_third(0)
     w_second(1)
     load_cot.wait()
-
-    def flip(b, carry):
-        cott[:, row_block(b)] = jnp.transpose(cot[row_block(b), :], (1, 0))
-        return carry
-
-    lax.fori_loop(0, NB, flip, 0)
-    w_third(0)
 
     scan_a, scan_b = scans[: len(scans) // 2], scans[len(scans) // 2 :]
     tot, ent = scan_a[0], scan_a[9]
@@ -688,6 +683,11 @@
                 )
 
     every = (0, 1, 2, 3)
+    def flip(b, carry):
+        cott[:, row_block(b)] = jnp.transpose(cot[row_block(b), :], (1, 0))
+        return carry
+
+    lax.fori_loop(0, NB, flip, 0)
     gw_term("0")
     mix(((0, every),), True, False)
     gw_first("0")
@@ -717,10 +717,13 @@
         back_states(n, grad_out)
         return carry
 
-    back_states(NB - 1, gf[...])
     for name in ("dr", "dl", "ar", "al"):
         rs[name].wait_recv()
     lax.fori_loop(0, NB - 1, back_rest, 0)
+    rows = slice((NB - 1) * BLOCK, REST)
+    grad_out = nn(cot[rows, :], wt[SLOT[0]])
+    grad_out = grad_out + from_r[rows, :].astype(f32) + from_l[rows, :].astype(f32)
+    back_states(NB - 1, jnp.concatenate([grad_out, gf[...]], axis=0))
     pair, along_y, along_x, back, done = scan_steps(scan_b, False)
 
     def back_intra(n, carry):

time: 112 us -> 114 us (1.018)
  Pallas kernels: 111 us -> 113 us
    pallas_call x1, Pallas kernels: 108 us -> 110 us  [on_device(): pl.pallas_call(kernel, out_shape=(jax.ShapeDtypeStruct((ROWS, FEAT), bf16...]
where the time goes in v6:
time: 114 us
  Pallas kernels  113 us (99%)
    pallas_call x1, Pallas kernels, on_device(): pl.pallas_call(kernel, out_shape=(jax.ShapeDtypeStruct((ROWS, FEAT), bf16...  110 us
    pallas_call x1, Pallas kernels, hand_over(): pl.pallas_call(hand_over_kernel, out_shape=tuple((jax.ShapeDtypeStruct(a....  3.14 us

profile of v6, /device:TPU:4, one launch (start us, length us, event | category | flops | bytes accessed | tf_op | source)
XLA Modules:
  0.0 113.7 jit_solution(12126268284174669971)
XLA Ops:
  0.6 109.8 %sublayer.1 = (bf16[1024,1024]{1,0:T(8,128)(2,1)}, bf16[64,1024]{1,0:T(8,128)(2,1)}, bf16[64,1024]{1,0:T(8,128)(2,1)}, bf16[1024,512]{1,0:T(8,128)(2,1)}, bf16[128,512]{1,0:T(8,128)(2,1)}) custom-call(bf16[64,1024]{1,0:T(8,128)(2,1)} %bitcast.5, bf16[64,1024]{1,0:T(8,128)(2,1)} %bitcast.6, f32[3,512]{1,0:T(4,128)} %cw_hbm.1, f32[1,512]{1,0:T(1,128)} %bitcast.7, ...), custom_call_target="tpu_custom_call" | custom-call | tf_op jit(solution)/shard_map/sublayer/pallas_call | solution.py:872
  110.4 3.1 %hand_over.1 = (bf16[1024,1024]{1,0:T(8,128)(2,1)}, bf16[64,1024]{1,0:T(8,128)(2,1)}, bf16[64,1024]{1,0:T(8,128)(2,1)}, bf16[1024,512]{1,0:T(8,128)(2,1)}, bf16[128,512]{1,0:T(8,128)(2,1)}) custom-call(bf16[1024,1024]{1,0:T(8,128)(2,1)} %get-tuple-element.15.refs_0_, bf16[64,1024]{1,0:T(8,128)(2,1)} %get-tuple-element.16.refs_1_, ...), custom_call_target="tpu_custom_call" | custom-call | tf_op jit(solution)/shard_map/hand_over/pallas_call | solution.py:856

commit v7 on v5

--- a/solution.py
+++ b/solution.py
@@ -803,7 +803,7 @@
     ag["f", 0].wait_recv()
     ag["f", 2].wait_recv()
     gw_term("2a")
-    mix(((1, every), (3, every)), False, False)
+    mix(((1, every), (3, every)), False, False, 0, 2)
     gw_second("3")
     gw_second("1")
     gw_first("2a")
@@ -812,13 +812,14 @@
     gw_term("2b", True)
     mix(((2, every),), False, True, 0, 2)
     gw_first("2b")
-    mix(((2, every),), False, True, 2, 4)
+    mix(((1, every), (3, every), (2, every)), False, True, 2, 3)
     gw_second("2a")
     gw_third("3")
     gw_move(3)
     gw_third("1")
     gw_move(1)
     gw_second("2b")
+    mix(((1, every), (3, every), (2, every)), False, True, 3, 4)
     gw_third("2a")
     gw_third("2b")
     gw_move(2)

time: 112 us -> 112 us (level)
  no operation moved by 1% of the time
where the time goes in v7:
time: 112 us
  Pallas kernels  111 us (99%)
    pallas_call x1, Pallas kernels, on_device(): pl.pallas_call(kernel, out_shape=(jax.ShapeDtypeStruct((ROWS, FEAT), bf16...  108 us
    pallas_call x1, Pallas kernels, hand_over(): pl.pallas_call(hand_over_kernel, out_shape=tuple((jax.ShapeDtypeStruct(a....  3.14 us

profile of v7, /device:TPU:4, one launch (start us, length us, event | category | flops | bytes accessed | tf_op | source)
XLA Modules:
  0.0 111.8 jit_solution(2482132771291317083)
XLA Ops:
  0.6 107.9 %sublayer.1 = (bf16[1024,1024]{1,0:T(8,128)(2,1)}, bf16[64,1024]{1,0:T(8,128)(2,1)}, bf16[64,1024]{1,0:T(8,128)(2,1)}, bf16[1024,512]{1,0:T(8,128)(2,1)}, bf16[128,512]{1,0:T(8,128)(2,1)}) custom-call(bf16[64,1024]{1,0:T(8,128)(2,1)} %bitcast.5, bf16[64,1024]{1,0:T(8,128)(2,1)} %bitcast.6, f32[3,512]{1,0:T(4,128)} %cw_hbm.1, f32[1,512]{1,0:T(1,128)} %bitcast.7, ...), custom_call_target="tpu_custom_call" | custom-call | tf_op jit(solution)/shard_map/sublayer/pallas_call | solution.py:870
  108.5 3.1 %hand_over.1 = (bf16[1024,1024]{1,0:T(8,128)(2,1)}, bf16[64,1024]{1,0:T(8,128)(2,1)}, bf16[64,1024]{1,0:T(8,128)(2,1)}, bf16[1024,512]{1,0:T(8,128)(2,1)}, bf16[128,512]{1,0:T(8,128)(2,1)}) custom-call(bf16[1024,1024]{1,0:T(8,128)(2,1)} %get-tuple-element.15.refs_0_, bf16[64,1024]{1,0:T(8,128)(2,1)} %get-tuple-element.16.refs_1_, ...), custom_call_target="tpu_custom_call" | custom-call | tf_op jit(solution)/shard_map/hand_over/pallas_call | solution.py:854
